TPU v7x, 32 devices: a whole 2x2x4 slice. The times are simulated.
32 devices in a mesh: dp: 16 (over z, y, core), mp: 2 (over x).
Axes of the slice: x: 2, y: 2, z: 4, core: 2. Of those that a mesh axis runs over, the one named last changes fastest.
Arguments:
- image_latents: bfloat16 [1024, 16, 16, 256], P('dp', None, None, 'mp'), may hold values from -6 to 6
- image_heights: int32 [1024], P('dp'), may hold values from 4 to 16, as said below
- code_index: int32 [1024, 16, 16], P('dp'), may hold values from 0 to 511
- kernel_three: bfloat16 [9, 256, 256], P(None, None, 'mp'), may hold values from -0.125 to 0.125
- bias_three: bfloat16 [256], P('mp'), may hold values from -3 to 3
- weight_mix: bfloat16 [256, 256], P('mp'), may hold values from -0.375 to 0.375
- bias_mix: bfloat16 [256], P('mp'), may hold values from -3 to 3
- weight_project: bfloat16 [256, 64], P('mp'), may hold values from -0.375 to 0.375
- bias_project: bfloat16 [64], replicated, may hold values from -3 to 3
- codebook: bfloat16 [512, 64], replicated, may hold values from -6 to 6
- weight_decode: bfloat16 [64, 256], P(None, 'mp'), may hold values from -0.75 to 0.75
- bias_decode: bfloat16 [256], P('mp'), may hold values from -3 to 3
- out_grad: bfloat16 [1024, 16, 16, 256], P('dp', None, None, 'mp'), may hold values from -6 to 6
Outputs:
- decoded: bfloat16 [1024, 16, 16, 256], P('dp', None, None, 'mp')
- latents_grad: bfloat16 [1024, 16, 16, 256], P('dp', None, None, 'mp')
- kernel_grad: float32 [9, 256, 256], P(None, None, 'mp')
- bias_three_grad: float32 [256], P('mp')
- mix_grad: float32 [256, 256], P('mp')
- bias_mix_grad: float32 [256], P('mp')
- project_grad: float32 [256, 64], P('mp')
- bias_project_grad: float32 [64], replicated
- codebook_grad: float32 [512, 64], replicated
- decode_grad: float32 [64, 256], P(None, 'mp')
- bias_decode_grad: float32 [256], P('mp')
Inputs may be any that keep to these rules, and one draw needn't show every extreme that they name: `image_heights`: at least one image has all 16 rows live and one has 4.
All inputs are finite; a program needn't handle non-finite values.
Results may differ from a plain program's by a relative error of at most 0.0054.
Values may be sent and summed in bfloat16 or wider, within the bound.
No kernel may reach another device: no remote copies, remote signals or barrier semaphores. Data moves between devices by JAX's collectives and lax.ppermute only.
A program may use at most 320 MiB of HBM per device.

v0:
```python
import functools

import jax
import jax.numpy as jnp
from jax import lax
from jax.experimental import pallas as pl
from jax.experimental.pallas import tpu as pltpu
from jax.sharding import PartitionSpec as P

SIDE = 16
HALF = 128
LEAD = 16
BLOCK = 32
TILE = 32
MARK = 1e9
GELU_SCALE = 0.7978845608028654
GELU_CUBE = 0.044715
COMMIT = 0.25
F32 = jnp.float32
BF16 = jnp.bfloat16
ANY = pl.BlockSpec(memory_space=pl.ANY)
SMEM = pl.BlockSpec(memory_space=pltpu.SMEM)
HBM = pl.BlockSpec(memory_space=pltpu.HBM)
VMEM = pl.BlockSpec(memory_space=pltpu.VMEM)
MIB = 1 << 20

NT = (((1,), (1,)), ((), ()))
TN = (((0,), (0,)), ((), ()))
NN = (((1,), (0,)), ((), ()))


def dot(a, b, dims=NN):
    return lax.dot_general(a, b, dims, preferred_element_type=F32)


def one_hot_columns(codes, code_of):
    return jnp.where(code_of == codes.astype(jnp.int16), jnp.bfloat16(1), jnp.bfloat16(0))


def numbers(count, width):
    return lax.broadcasted_iota(jnp.int32, (count, width), 0).astype(jnp.int16)


def shape(dims, kind):
    return jax.ShapeDtypeStruct(dims, kind)


def params(mib):
    return pltpu.CompilerParams(vmem_limit_bytes=mib * MIB)


def cost(flops, moved, slow=0):
    return pl.CostEstimate(flops=flops, bytes_accessed=moved, transcendentals=slow)


class Plan:
    def __init__(self, images):
        self.images = images
        longest = images * SIDE // 2 + SIDE // 2
        part = images // 8
        self.chunks = [19 * part, 28 * part]
        self.usual = len(self.chunks)
        rest = longest - sum(self.chunks)
        self.chunks.append(rest)
        self.starts = [sum(self.chunks[:k]) for k in range(len(self.chunks))]
        self.total = sum(self.chunks)
        self.packed = -(-(LEAD + longest + self.total + LEAD) // SIDE) * SIDE
        self.rows, self.block = [], []
        for k, c in enumerate(self.chunks):
            block = BLOCK if k < self.usual else SIDE
            most = 1 + c + 15 + c // 4 + 1
            self.rows.append(-(-most // block) * block)
            self.block.append(block)
        self.covered = sum(self.chunks[: self.usual])


def meta_size(plan):
    return plan.images + len(plan.chunks) + 1 + 5


def plan_rows(plan, heights, place, meta):
    images = plan.images
    base = images + len(plan.chunks) + 1

    def total_of(b, acc):
        return acc + heights[b]

    total = lax.fori_loop(0, images, total_of, jnp.int32(0))

    def split_of(b, state):
        acc, best, split, cut = state
        acc = acc + heights[b]
        worst = jnp.maximum(acc, total - acc)
        better = worst < best
        return (acc, jnp.where(better, worst, best), jnp.where(better, b + 1, split), jnp.where(better, acc, cut))

    _, _, split, cut = lax.fori_loop(0, images, split_of, (jnp.int32(0), jnp.int32(1 << 20), jnp.int32(0), jnp.int32(0)))
    mine = place[0]
    own_first = jnp.where(mine == 0, 0, split)
    own_last = jnp.where(mine == 0, split, images)
    own_row = jnp.where(mine == 0, 0, cut)
    send_row = jnp.where(mine == 0, cut, 0)
    for k in range(len(plan.chunks) + 1):
        meta[images + k] = own_first
    ends = [plan.starts[k] + plan.chunks[k] for k in range(len(plan.chunks))]

    def place_of(b, acc):
        meta[b] = acc - own_row
        acc = acc + heights[b]
        end = acc - own_row
        inside = jnp.logical_and(b >= own_first, b < own_last)
        step = jnp.int32(0)
        for k in range(len(plan.chunks) - 1):
            step = step + (end > ends[k]).astype(jnp.int32)

        @pl.when(inside)
        def _():
            meta[images + 1 + step] = b + 1

        return acc

    lax.fori_loop(0, images, place_of, jnp.int32(0))
    for k in range(len(plan.chunks)):
        meta[images + k + 1] = jnp.maximum(meta[images + k + 1], meta[images + k])
    meta[base] = own_row
    meta[base + 1] = send_row
    meta[base + 2] = own_first
    meta[base + 3] = own_last
    meta[base + 4] = jnp.maximum(cut, total - cut)


def pack_rows(plan, meta, source, packed, piece, count):
    base = plan.images + len(plan.chunks) + 1

    def one(i, carry):
        b = piece * count + i
        row = meta[b] + meta[base] + LEAD
        packed[pl.ds(row, SIDE)] = source[b]
        return carry

    lax.fori_loop(0, count, one, 0)


def pack_latents(plan, heights, place, x_hbm, _, meta, own, *rest):
    n = len(plan.chunks)
    sends, (x_in, packed, sem_in, sem_out) = rest[:n], rest[n:]
    pieces = 8
    count = plan.images // pieces
    fetch = []
    for p in range(pieces):
        part = pl.ds(p * count, count)
        fetch.append(pltpu.make_async_copy(x_hbm.at[part], x_in.at[part], sem_in.at[p]))
        fetch[-1].start()
    plan_rows(plan, heights, place, meta)
    base = plan.images + n + 1
    for p in range(pieces):
        fetch[p].wait()
        pack_rows(plan, meta, x_in, packed, p, count)
    copies = []
    for k in range(n):
        part = pl.ds(LEAD + meta[base + 1] + plan.starts[k], plan.chunks[k])
        copies.append(pltpu.make_async_copy(packed.at[part], sends[k], sem_out.at[k]))
        copies[-1].start()
    copies.append(pltpu.make_async_copy(packed.at[pl.ds(meta[base], LEAD + plan.total)], own, sem_out.at[n]))
    copies[-1].start()
    for copy in copies:
        copy.wait()


def pack_code_grads(plan, meta, og_hbm, *rest):
    n = len(plan.chunks)
    sources, (own, small), rest = rest[:5], rest[6:8], rest[8:]
    sends, rest = rest[:n], rest[n:]
    og_in, packed, sem_in, sem_small = rest[:4]
    held = rest[4:]
    small_fetch = []
    for i in range(5):
        small_fetch.append(pltpu.make_async_copy(sources[i], held[i], sem_small.at[i]))
        small_fetch[-1].start()
    decode_w, weight_mix, project_t, bias_first, bias_mix = held
    pieces = 8
    count = plan.images // pieces
    fetch = []
    for p in range(pieces):
        part = pl.ds(p * count, count)
        fetch.append(pltpu.make_async_copy(og_hbm.at[part], og_in.at[part], sem_in.at[p]))
        fetch[-1].start()
    base = plan.images + n + 1

    def clear(i, carry):
        packed[pl.ds(i * SIDE, SIDE)] = jnp.zeros((SIDE, SIDE, HALF), BF16)
        return carry

    lax.fori_loop(0, packed.shape[0] // SIDE, clear, 0)
    for copy in small_fetch:
        copy.wait()
    side = HALF // 2
    small[0:HALF] = weight_mix[:, :HALF]
    small[HALF : 2 * HALF] = weight_mix[:, HALF:]
    small[2 * HALF : 2 * HALF + side] = project_t[...]
    which = lax.broadcasted_iota(jnp.int32, (SIDE, HALF), 0)
    first, second = bias_first[...].astype(F32), bias_mix[...].astype(F32)
    first = jnp.where(which == 0, first, jnp.where(which == 1, second, 0.0))
    small[2 * HALF + side : 2 * HALF + side + SIDE] = first.astype(BF16)
    w = decode_w[...]
    blank = jnp.zeros_like(w)
    upper = jnp.concatenate([w, blank], axis=0)
    lower = jnp.concatenate([blank, w], axis=0)
    for p in range(pieces):
        fetch[p].wait()
        pack_rows(plan, meta, og_in, packed, p, count)
    for k in range(n):
        half = plan.chunks[k] // 2
        for which in range(2):
            row = LEAD + meta[base + 1 - which] + plan.starts[k]
            a = packed[pl.ds(row, half)].reshape(half * SIDE, HALF)
            b = packed[pl.ds(row + half, half)].reshape(half * SIDE, HALF)
            both = dot(a, upper, NT) + dot(b, lower, NT)
            both = both.reshape(half, SIDE, HALF)
            if which == 0:
                sends[k][...] = both.astype(BF16)
            else:
                own[pl.ds(plan.starts[k] // 2, half)] = both


def prepare_weights(place, own_hbm, far_hbm, far_other_hbm, small, far_small, bias_code, codebook_t, *refs):
    forward, backward, mix, project, bias, book, kernel, far_kernel, sems = refs
    copies = []
    halves = [pl.ds(pl.multiple_of(at * HALF, HALF), HALF) for at in (place[1], 1 - place[1])]
    pairs = [(own_hbm, kernel)]
    pairs += [(source, far_kernel.at[:, rows, :]) for source, rows in zip((far_hbm, far_other_hbm), halves)]
    for i, (source, target) in enumerate(pairs):
        copies.append(pltpu.make_async_copy(source, target, sems.at[i]))
        copies[-1].start()
    for copy in copies:
        copy.wait()
    first = pl.multiple_of(place[0] * HALF, HALF)
    order = (first, HALF - first)
    for tap in range(9):
        for d, source in enumerate((kernel, far_kernel)):
            for c in range(2):
                tile = source[tap, pl.ds(order[c], HALF), :]
                row = tap * 2 * HALF
                forward[row + c * HALF : row + (c + 1) * HALF, d * HALF : (d + 1) * HALF] = tile
                backward[row + d * HALF : row + (d + 1) * HALF, c * HALF : (c + 1) * HALF] = tile.T
    blank = jnp.zeros((HALF, HALF // 2), BF16)
    for d, source in enumerate((small, far_small)):
        rows = pl.ds(d * HALF, HALF)
        for c in range(2):
            mix[rows, c * HALF : (c + 1) * HALF] = source[pl.ds(order[c], HALF), :]
        part = source[2 * HALF : 2 * HALF + HALF // 2, :].T
        project[0, rows, :] = jnp.concatenate([part, blank], axis=1)
        project[1, rows, :] = jnp.concatenate([blank, part], axis=1)
        bias[0:8, d * HALF : (d + 1) * HALF] = source[2 * HALF + HALF // 2 : 2 * HALF + HALF // 2 + SIDE, :].astype(F32)[0:8]
    code = bias_code[...].astype(F32)
    code = jnp.concatenate([code, code], axis=1)
    bias[8:16, :] = jnp.broadcast_to(jnp.concatenate([code, code], axis=1), (8, 2 * HALF))
    book[...] = jnp.concatenate([codebook_t[...], codebook_t[...]], axis=0)


def sum_codes(first, group, heights, codes, og, codebook_t, _, __, grads, hot, cots, sums):
    step = pl.program_id(0)

    @pl.when(step == 0)
    def _():
        sums[...] = jnp.zeros_like(sums)

    spots = SIDE * SIDE
    code_of = numbers(codebook_t.shape[1], spots)
    spot = lax.broadcasted_iota(jnp.int32, (spots, 1), 0)
    for i in range(group):
        live = heights[(first + step) * group + i] * SIDE
        hot[:, i * spots : (i + 1) * spots] = one_hot_columns(codes[i : i + 1, :], code_of)
        cot = og[i].reshape(spots, HALF).astype(F32)
        cots[i * spots : (i + 1) * spots] = jnp.where(spot < live, cot, 0.0).astype(BF16)
    half = sums.shape[0] // 2
    for h in (0, half):
        sums[h : h + half] += dot(hot[h : h + half], cots[...])

    @pl.when(step == pl.num_programs(0) - 1)
    def _():
        total = sums[...]
        book = codebook_t[...].astype(F32)
        w = lax.dot_general(book, total, NN, precision=lax.Precision.HIGHEST, preferred_element_type=F32)
        bias = jnp.sum(total, axis=0, keepdims=True)
        embed = w.shape[0]
        grads[0:embed] = w
        grads[embed : embed + 8] = jnp.broadcast_to(bias, (8, HALF))


def decode_images(plan, steps, heights, codes, codebook_t, decode_w, decode_b, _, decoded, token, table):
    step = pl.program_id(0)
    token[...] = jnp.zeros_like(token)
    group = plan.images // steps

    @pl.when(step == 0)
    def _():
        full = dot(codebook_t[...], decode_w[...], TN) + decode_b[...].astype(F32)
        table[...] = full.T.astype(BF16)

    spots = SIDE * SIDE
    code_of = numbers(codebook_t.shape[1], spots)
    spot = lax.broadcasted_iota(jnp.int32, (spots, 1), 0)
    for i in range(group):
        live = heights[step * group + i] * SIDE
        out = dot(table[...], one_hot_columns(codes[i : i + 1, :], code_of)).T
        decoded[i] = jnp.where(spot < live, out, 0.0).astype(BF16).reshape(SIDE, SIDE, HALF)


def put_codes(code_rows, codes, b, height, dst):
    spot = lax.broadcasted_iota(jnp.int32, (1, SIDE * SIDE), 1)
    lane = lax.broadcasted_iota(jnp.int32, (1, HALF), 1)
    per_row = HALF // SIDE
    row = jnp.where(spot < height * SIDE, codes[pl.ds(b, 1), :], -1)
    turn = lax.rem(dst, per_row) * SIDE
    upper = pltpu.roll(row[:, :HALF], turn, 1)
    lower = pltpu.roll(row[:, HALF:], turn, 1)
    inside = lane >= turn
    pieces = (jnp.where(inside, upper, -1), jnp.where(inside, lower, upper), jnp.where(inside, -1, lower))
    for i, piece in enumerate(pieces):
        target = pl.ds(dst // per_row + i, 1)
        code_rows[target, :] = jnp.where(piece < 0, code_rows[target, :], piece)


def gelu_parts(v):
    square = v * v
    t = jnp.tanh(v * (GELU_SCALE + (GELU_SCALE * GELU_CUBE) * square))
    half = 0.5 + 0.5 * t
    value = v * half
    slope = half + (value - value * half) * (2.0 * GELU_SCALE + (6.0 * GELU_SCALE * GELU_CUBE) * square)
    return value, slope


def main_step(plan, layout, k, waits, *refs):
    first_step = k == 0
    fresh = k in (0, plan.usual)
    final = k == plan.usual - 1
    refs = list(refs[waits:])

    def take(count):
        got = refs[:count]
        del refs[:count]
        return got

    if final:
        place, decode_acc = take(2)
    meta, heights, x_own, x_far, q_own, q_far, codes = take(7)
    kernel_hbm, kernel_t_hbm, mix, project, bias, book = take(6)
    if not first_step:
        x_past, q_past, carry_own, carry_far = take(4)
    if not fresh:
        past_accs = take(5)
    win_own, win_far, next_own, next_far = take(4)
    if final:
        laid_out = take(3)
    if not final:
        sums_out = take(5)
    kernel_acc, mix_acc, project_acc, book_acc, bias_acc = take(5)
    kernel, kernel_t, weight_sems = take(3)
    xo, xf, qo, qf, qd, xc_o, xc_f, qc, code_rows, act3, slope_x, grad3, block_g = take(13)
    second_s, slope_s, low_s, mixed_s, code_s, hot_s, found_s, diff_s, sems = refs

    chunk, start = plan.chunks[k], plan.starts[k]
    images, rows, block = plan.images, plan.rows[k], plan.block[k]
    half = chunk // 2
    spots = block * SIDE
    low = meta[images + k]
    high = meta[images + k + 1]

    copies = [
        (x_own.at[pl.ds(start, LEAD + chunk)], xo.at[pl.ds(0, LEAD + chunk)]),
        (x_far, xf.at[pl.ds(LEAD, chunk)]),
        (q_own.at[pl.ds(start // 2, half)], qo.at[pl.ds(LEAD, half)]),
        (q_far, qf.at[pl.ds(LEAD, half)]),
    ]
    if not first_step:
        past = plan.chunks[k - 1]
        copies += [
            (x_past.at[pl.ds(past - LEAD, LEAD)], xf.at[pl.ds(0, LEAD)]),
            (q_own.at[pl.ds(start // 2 - LEAD, LEAD)], qo.at[pl.ds(0, LEAD)]),
            (q_past.at[pl.ds(past // 2 - LEAD, LEAD)], qf.at[pl.ds(0, LEAD)]),
        ]
    accs = (mix_acc, project_acc, book_acc, bias_acc, kernel_acc)
    early = len(copies)
    if not fresh:
        copies += list(zip(past_accs[1:] + past_accs[:1], accs))
    weight_copies = []
    for i, (source, target) in enumerate(((kernel_hbm, kernel), (kernel_t_hbm, kernel_t))):
        weight_copies.append(pltpu.make_async_copy(source, target, weight_sems.at[i]))
    started = []
    for i, (source, target) in enumerate(copies):
        started.append(pltpu.make_async_copy(source, target, sems.at[i]))
        started[-1].start()
    for copy in weight_copies:
        copy.start()
    started, later = started[:early], started[early:]

    if fresh:
        for acc in accs:
            acc[...] = jnp.zeros(acc.shape, F32)

    blank = jnp.zeros((SIDE, SIDE, HALF), BF16)
    no_row = jnp.full((SIDE, SIDE, HALF), MARK, F32)
    code_rows[...] = jnp.full(code_rows.shape, -1, jnp.int32)
    for r in range(0, rows + 2 * block, SIDE):
        part = pl.ds(r, SIDE)
        xc_o[part] = blank
        xc_f[part] = blank
        if r < rows:
            qc[part] = no_row
    for copy in started:
        copy.wait()

    lane3 = lax.broadcasted_iota(jnp.int32, (1, SIDE, HALF), 2) < HALF // 2

    def spread(r0, count):
        both = (qo[pl.ds(r0, count)] + qf[pl.ds(r0, count)].astype(F32)).reshape(count * SIDE, HALF)
        turned = pltpu.roll(both, HALF // 2, 1).reshape(count, SIDE, HALF)
        both = both.reshape(count, SIDE, HALF)
        return jnp.where(lane3, both, turned), jnp.where(lane3, turned, both)

    upper, lower = spread(LEAD, half)
    qd[pl.ds(LEAD, half)] = upper
    qd[pl.ds(LEAD + half, half)] = lower
    if not first_step:
        _, lower = spread(0, LEAD)
        qd[0:LEAD] = lower

    per_row = HALF // SIDE

    def put(b, dst):
        src = meta[b] - start + LEAD
        xc_o[pl.ds(dst, SIDE)] = xo[pl.ds(src, SIDE)]
        xc_f[pl.ds(dst, SIDE)] = xf[pl.ds(src, SIDE)]
        qc[pl.ds(dst, SIDE)] = qd[pl.ds(src, SIDE)]
        end = dst + heights[b]
        xc_o[pl.ds(end, SIDE)] = blank
        xc_f[pl.ds(end, SIDE)] = blank
        qc[pl.ds(end, SIDE)] = no_row
        put_codes(code_rows, codes, b, heights[b], dst)
        return end + 1

    used = lax.fori_loop(low, high, put, jnp.int32(1))
    blocks = jnp.where(high > low, (used + (block - 1)) // block, 0)

    column = lax.rem(lax.broadcasted_iota(jnp.int32, (TILE, 1), 0), SIDE)
    not_first = column != 0
    not_last = column != SIDE - 1

    def shifted(value):
        back = jnp.where(not_first, pltpu.roll(value, 1, 0), 0.0)
        ahead = jnp.where(not_last, pltpu.roll(value, TILE - 1, 0), 0.0)
        return back.astype(BF16), ahead.astype(BF16)

    edge = jnp.zeros((SIDE, 3 * 2 * HALF), BF16)
    act3[0:SIDE] = edge
    grad3[0:SIDE] = edge
    beyond = pl.multiple_of((blocks * block + 1) * SIDE, SIDE)
    grad3[pl.ds(beyond, SIDE)] = edge

    tiles = range(0, spots, TILE)

    def read_x(r0, t):
        part = pl.ds(r0 + t // SIDE, TILE // SIDE)
        o = xc_o[part].reshape(TILE, HALF)
        f = xc_f[part].reshape(TILE, HALF)
        return jnp.concatenate([o, f], axis=1).astype(F32)

    def at(row, count=block):
        return pl.ds(pl.multiple_of(row * SIDE, SIDE), count * SIDE)

    def tile_at(row, t):
        return pl.ds(pl.multiple_of(row * SIDE, SIDE) + t, TILE)

    def activate(j, carry):
        r0 = j * block
        for t in tiles:
            value, slope = gelu_parts(read_x(r0, t))
            slope_x[tile_at(r0, t), :] = slope
            back, ahead = shifted(value)
            act3[tile_at(r0 + 1, t), 0 : 2 * HALF] = back
            act3[tile_at(r0 + 1, t), 2 * HALF : 4 * HALF] = value.astype(BF16)
            act3[tile_at(r0 + 1, t), 4 * HALF : 6 * HALF] = ahead
        return carry

    fused = k < plan.usual
    lax.fori_loop(0, 2 if fused else blocks + 1, activate, 0)
    for copy in later:
        copy.wait()
    for copy in weight_copies:
        copy.wait()

    bias_first = bias[0:1, :]
    bias_mix = bias[1:2, :]
    bias_code = bias[8:9, 0:HALF]
    lane = lax.broadcasted_iota(jnp.int32, (1, HALF), 1) < HALF // 2
    hb = block // 2
    hs = hb * SIDE

    def add_rows(total, value):
        for i in range(0, value.shape[0], 8):
            part = value[i : i + 8]
            total = part if total is None else total + part
        return total

    half_tiles = range(0, hs, TILE)
    code_of = numbers(book_acc.shape[0], HALF)
    halves = (0, hs)

    def middle(j, carry):
        r0 = j * block
        for i in range(block // per_row):
            row = code_rows[pl.ds(j * (block // per_row) + i, 1), :]
            hot_s[:, i * HALF : (i + 1) * HALF] = one_hot_columns(row, code_of)
        for h in halves:
            found_s[h : h + hs] = dot(book[...], hot_s[:, h : h + hs]).astype(BF16).T
        pre = []
        for h in halves:
            window = jnp.concatenate([act3[at(r0 + i + h // SIDE, hb), :] for i in range(3)], axis=1)
            pre.append(dot(window, kernel[...]))
        for h, part in zip(halves, pre):
            for t in half_tiles:
                value, slope = gelu_parts(part[t : t + TILE] + bias_first)
                second_s[h + t : h + t + TILE] = value.astype(BF16)
                slope_s[h + t : h + t + TILE] = slope
        mixed = [dot(second_s[h : h + hs], mix[...]) for h in halves]
        for h, part in zip(halves, mixed):
            for t in half_tiles:
                low_s[h + t : h + t + TILE] = (read_x(r0, h + t) + part[t : t + TILE] + bias_mix).astype(BF16)
        latents = [dot(low_s[h : h + hs], project[i]) for i, h in enumerate(halves)]
        total = None
        for t in half_tiles:
            first = pl.ds(r0 + t // SIDE, TILE // SIDE)
            other = pl.ds(r0 + hb + t // SIDE, TILE // SIDE)
            ch = jnp.where(lane, found_s[t : t + TILE].astype(F32), found_s[hs + t : hs + t + TILE].astype(F32))
            q = jnp.where(lane3, qc[first], qc[other]).reshape(TILE, HALF)
            live = q < 0.5 * MARK
            latent = latents[0][t : t + TILE] + latents[1][t : t + TILE] + bias_code
            diff = jnp.where(live, latent - ch, 0.0)
            code_grad = jnp.where(live, q + (2.0 * COMMIT) * diff, 0.0)
            code_s[t : t + TILE] = code_grad.astype(BF16)
            total = add_rows(total, code_grad)
            big = diff.astype(BF16).astype(F32)
            small = diff - big
            turned = pltpu.roll(small, HALF // 2, 1)
            diff_s[t : t + TILE] = jnp.where(lane, big, turned).astype(BF16)
            turned = pltpu.roll(big, HALF // 2, 1)
            diff_s[hs + t : hs + t + TILE] = jnp.where(lane, turned, small).astype(BF16)
        bias_acc[16:24, 0:HALF] += total
        total = None
        blocks_g = [dot(code_s[...], project[i], NT) for i in range(2)]
        for h, part in zip(halves, blocks_g):
            for t in half_tiles:
                block_g[tile_at(r0, h + t), :] = part[t : t + TILE]
                mixed_s[h + t : h + t + TILE] = part[t : t + TILE].astype(BF16)
                total = add_rows(total, part[t : t + TILE])
        bias_acc[8:16] += total
        second_grad = [dot(mixed_s[h : h + hs], mix[...], NT) for h in halves]
        total = None
        for h, part in zip(halves, second_grad):
            for t in half_tiles:
                first_grad = slope_s[h + t : h + t + TILE] * part[t : t + TILE]
                back, ahead = shifted(first_grad)
                grad3[tile_at(r0 + 1, h + t), 0 : 2 * HALF] = ahead
                grad3[tile_at(r0 + 1, h + t), 2 * HALF : 4 * HALF] = first_grad.astype(BF16)
                grad3[tile_at(r0 + 1, h + t), 4 * HALF : 6 * HALF] = back
                total = add_rows(total, first_grad)
        bias_acc[0:8] += total
        book_acc[...] += dot(hot_s[...], diff_s[...])
        mix_acc[...] += dot(second_s[...], mixed_s[...], TN)
        project_acc[...] += jnp.where(lane, dot(low_s[0:hs], code_s[...], TN), dot(low_s[hs:], code_s[...], TN))
        return carry

    def finish(j, carry):
        r0 = j * block
        active = act3[at(r0 + 1), 2 * HALF : 4 * HALF].T
        for i in range(3):
            kernel_acc[:, i * 6 * HALF : (i + 1) * 6 * HALF] += dot(active, grad3[at(r0 + 2 - i), :])
        grads = []
        for h in halves:
            window = jnp.concatenate([grad3[at(r0 + 2 - i + h // SIDE, hb), :] for i in range(3)], axis=1)
            grads.append(dot(window, kernel_t[...]))
        for h, grad in zip(halves, grads):
            for t in half_tiles:
                here = tile_at(r0, h + t)
                out = (block_g[here, :] + slope_x[here, :] * grad[t : t + TILE]).astype(BF16)
                part = pl.ds(r0 + (h + t) // SIDE, TILE // SIDE)
                xc_o[part] = out[:, :HALF].reshape(TILE // SIDE, SIDE, HALF)
                xc_f[part] = out[:, HALF:].reshape(TILE // SIDE, SIDE, HALF)
        return carry

    def opening(j, carry):
        middle(j, carry)
        return activate(j + 2, carry)

    def steady(j, carry):
        finish(j - 2, carry)
        middle(j, carry)
        return activate(j + 2, carry)

    if fused:
        lax.fori_loop(0, jnp.minimum(blocks, 2), opening, 0)
        lax.fori_loop(2, blocks, steady, 0)
        lax.fori_loop(jnp.maximum(blocks - 2, 0), blocks, finish, 0)
    else:
        lax.fori_loop(0, blocks, middle, 0)
        lax.fori_loop(0, blocks, finish, 0)
    leaving = []
    if not final:
        leaving += list(zip((kernel_acc, mix_acc, project_acc, book_acc, bias_acc), sums_out))
        for i, (source, target) in enumerate(leaving):
            leaving[i] = pltpu.make_async_copy(source, target, sems.at[i])
            leaving[i].start()

    out_o, out_f = xo, xf
    if first_step:
        out_o[0:LEAD] = blank
        out_f[0:LEAD] = blank
    else:
        out_o[0:LEAD] = carry_own[...]
        out_f[0:LEAD] = carry_far[...]

    def collect(b, src):
        dst = meta[b] - start + LEAD
        out_o[pl.ds(dst, SIDE)] = xc_o[pl.ds(src, SIDE)]
        out_f[pl.ds(dst, SIDE)] = xc_f[pl.ds(src, SIDE)]
        return src + heights[b] + 1

    lax.fori_loop(low, high, collect, jnp.int32(1))
    size = win_own.shape[0]
    windows = (
        (out_o.at[pl.ds(0, size)], win_own),
        (out_f.at[pl.ds(0, size)], win_far),
        (out_o.at[pl.ds(chunk, LEAD)], next_own),
        (out_f.at[pl.ds(chunk, LEAD)], next_far),
    )
    for i, (source, target) in enumerate(windows):
        leaving.append(pltpu.make_async_copy(source, target, sems.at[5 + i]))
        leaving[-1].start()
    if final:
        sums = (kernel_acc, mix_acc, project_acc, book_acc, bias_acc, decode_acc)
        laid_out += [slope_x.at[pl.ds(0, layout.rows), pl.ds(i * HALF, HALF)] for i in range(2)]
        leaving += gather_grads(plan, layout, place, meta, sums, *laid_out, sems)
    for copy in leaving:
        copy.wait()


class Layout:
    def __init__(self, devices, book_rows, embed):
        self.mix = 9 * 2 * HALF
        self.project = self.mix + 2 * HALF
        self.book = self.project + HALF // 2
        self.bias = self.book + book_rows // 2
        self.decode = self.bias + 8
        used = self.decode + embed + 8
        self.devices = devices
        self.piece = -(-used // (devices * SIDE)) * SIDE
        self.rows = self.piece * devices
        self.half = self.rows // 2
        self.used = used


def lay_out(layout, swap, kernel_acc, mix_acc, project_acc, book_acc, bias_acc, decode_acc, own, far):
    def lanes(value):
        return value[:, :HALF], value[:, HALF:]

    def order(first, second):
        return jnp.where(swap, second, first), jnp.where(swap, first, second)

    row = 0
    for tap in range(9):
        block = kernel_acc[:, tap * 2 * HALF : (tap + 1) * 2 * HALF]
        mine, theirs = lanes(block)
        a, b = order(mine[:HALF], mine[HALF:])
        own[row : row + HALF] = a
        own[row + HALF : row + 2 * HALF] = b
        a, b = order(theirs[:HALF], theirs[HALF:])
        far[row : row + HALF] = a
        far[row + HALF : row + 2 * HALF] = b
        row += 2 * HALF
    row = layout.mix
    for target, part in ((own, mix_acc[:HALF]), (far, mix_acc[HALF:])):
        a, b = order(*lanes(part))
        target[row : row + HALF] = a
        target[row + HALF : row + 2 * HALF] = b
    row = layout.project
    side = HALF // 2
    for target, part in ((own, project_acc[:HALF]), (far, project_acc[HALF:])):
        part = part + pltpu.roll(part, side, 1)
        target[row : row + side] = part.T[:side]
    row = layout.book
    book = book_acc[...]
    book = -2.0 * (book + pltpu.roll(book, side, 1))
    book = book.T[:side]
    for c in range(book.shape[1] // HALF):
        part = book[:, c * HALF : (c + 1) * HALF]
        own[row + c * side : row + (c + 1) * side] = part
        far[row + c * side : row + (c + 1) * side] = part
    row = layout.bias
    sums = [jnp.sum(bias_acc[8 * i : 8 * i + 8], axis=0, keepdims=True) for i in range(3)]
    code = sums[2][:, :HALF]
    code = code + pltpu.roll(code, side, 1)
    which = lax.broadcasted_iota(jnp.int32, (8, HALF), 0)
    for target, first in ((own, 0), (far, HALF)):
        part = jnp.where(which == 0, sums[0][:, first : first + HALF], sums[1][:, first : first + HALF])
        target[row : row + 8] = jnp.where(which == 2, code, jnp.where(which < 2, part, 0.0))
    row = layout.decode
    rest = layout.rows - row
    own[row:] = jnp.zeros((rest, HALF), F32)
    far[row:] = jnp.zeros((rest, HALF), F32)
    if decode_acc is not None:
        own[row : row + decode_acc.shape[0]] = decode_acc[...]


def gather_plain(layout, place, *refs):
    lay_out(layout, place[0] == 1, *refs[:5], None, *refs[5:])


def gather_grads(plan, layout, place, meta, accs, keep_own, keep_far, send, own, far, sems):
    lay_out(layout, place[0] == 1, *accs, own, far)
    base = plan.images + len(plan.chunks) + 1
    over = (meta[base + 4] > plan.covered).astype(F32)
    which = lax.broadcasted_iota(jnp.int32, (8, HALF), 0)
    row = layout.bias
    own[row : row + 8] = jnp.where(which == 3, over, own[row : row + 8])
    half = layout.half
    mine = pl.ds(pl.multiple_of(place[1] * half, SIDE), half)
    other = pl.ds(pl.multiple_of((1 - place[1]) * half, SIDE), half)
    kept = []
    for i, (source, target) in enumerate(((own, keep_own), (far, keep_far))):
        kept.append(pltpu.make_async_copy(source.at[mine, :], target, sems.at[9 + i]))
        kept[-1].start()
    send[0] = own[other, :].astype(BF16)
    send[1] = far[other, :].astype(BF16)
    return kept


def hold(*refs):
    pass


def add_far(keep_far, came, out):
    out[...] = (keep_far[...] + came[1].astype(F32)).astype(BF16)


def add_own(keep_own, came, came_far, out, token):
    token[...] = jnp.zeros_like(token)
    total = keep_own[...] + came[0].astype(F32) + came_far[...].astype(F32)
    out[...] = total.astype(BF16).reshape(out.shape)


def add_pieces(pieces, _, out, token):
    token[...] = jnp.zeros_like(token)
    total = pieces[0].astype(F32)
    for i in range(1, pieces.shape[0]):
        total = total + pieces[i].astype(F32)
    out[...] = jnp.broadcast_to(total.astype(BF16)[None], out.shape)


def write_grads(layout, place, mine, theirs, kernel, first_bias, mix, mix_bias, project, project_bias, book, decode, decode_bias, whole):
    half = layout.half
    whole[pl.ds(pl.multiple_of(place[1] * half, SIDE), half), :] = mine[...].astype(F32)
    whole[pl.ds(pl.multiple_of((1 - place[1]) * half, SIDE), half), :] = theirs[...].astype(F32)
    split_grads(layout, whole, kernel, first_bias, mix, mix_bias, project, project_bias, book, decode, decode_bias)


def split_grads(layout, whole, kernel, first_bias, mix, mix_bias, project, project_bias, book, decode, decode_bias):
    for tap in range(9):
        kernel[tap] = whole[tap * 2 * HALF : (tap + 1) * 2 * HALF]
    row = layout.mix
    mix[:, :HALF] = whole[row : row + HALF]
    mix[:, HALF:] = whole[row + HALF : row + 2 * HALF]
    side = HALF // 2
    for row, target in ((layout.project, project), (layout.book, book)):
        for c in range(target.shape[1] // HALF):
            target[:, c * HALF : (c + 1) * HALF] = whole[row + c * side : row + (c + 1) * side]
    row = layout.bias
    first_bias[...] = whole[row : row + 1]
    mix_bias[...] = whole[row + 1 : row + 2]
    project_bias[...] = whole[row + 2 : row + 3, :side]
    row = layout.decode
    n = decode.shape[0]
    decode[...] = whole[row : row + n]
    decode_bias[...] = whole[row + n : row + n + 1]


def split_again(layout, total, extra, *refs):
    whole = refs[-1]
    whole[...] = total[...].astype(F32) + extra[...]
    split_grads(layout, whole, *refs[:-1])


def restore_rows(plan, n, waits, *refs):
    meta, heights, *refs = refs[waits:]
    own, far, out, token = refs[:n], refs[n : 2 * n], refs[2 * n], refs[2 * n + 1]
    token[...] = jnp.zeros_like(token)
    stage_own, stage_far, sems = refs[2 * n + 2 :]
    copies = []
    for k in range(n):
        size = plan.chunks[k] + (LEAD if k == n - 1 else 0)
        for i, (source, target) in enumerate(((own[k], stage_own), (far[k], stage_far))):
            from_rows = source.at[pl.ds(0, size)]
            copies.append(pltpu.make_async_copy(from_rows, target.at[pl.ds(plan.starts[k], size)], sems.at[i, k]))
            copies[-1].start()
    for copy in copies:
        copy.wait()
    base = plan.images + len(plan.chunks) + 1
    own_row, send_row = meta[base], meta[base + 1]
    first, last = meta[base + 2], meta[base + 3]
    row_of = lax.broadcasted_iota(jnp.int32, (SIDE, 1, 1), 0)

    def own_image(b, carry):
        rows = stage_own[pl.ds(meta[b] + LEAD, SIDE)]
        out[b] = jnp.where(row_of < heights[b], rows, jnp.zeros_like(rows))
        return carry

    def far_image(b, carry):
        rows = stage_far[pl.ds(meta[b] + own_row - send_row + LEAD, SIDE)]
        out[b] = jnp.where(row_of < heights[b], rows, jnp.zeros_like(rows))
        return carry

    lax.fori_loop(first, last, own_image, 0)
    lax.fori_loop(0, first, far_image, 0)
    lax.fori_loop(last, plan.images, far_image, 0)


def trade(value):
    return lax.ppermute(value, "mp", [(0, 1), (1, 0)])


def held(value, *others):
    return pl.pallas_call(
        hold,
        out_shape=shape(value.shape, value.dtype),
        in_specs=[ANY] * (1 + len(others)),
        out_specs=ANY,
        input_output_aliases={0: 0},
        compiler_params=params(60),
        name="hold",
    )(value, *others)


def run_main(plan, layout, k, meta, heights, streams, weights, state, waits=(), ending=()):
    chunk, rows, block = plan.chunks[k], plan.rows[k], plan.block[k]
    last = k >= plan.usual - 1
    final = k == plan.usual - 1
    x_own, x_far, q_own, q_far, codes = streams
    book_rows = weights[-1].shape[1]
    args = [*waits, *ending, meta, heights, x_own, x_far[k], q_own, q_far[k], codes, *weights]
    specs = [ANY] * len(waits) + ([SMEM, VMEM] if final else [])
    specs += [SMEM, SMEM, ANY, ANY, ANY, ANY, VMEM, ANY, ANY] + [VMEM] * (len(weights) - 2)
    alias = {}
    if state is not None:
        args += [x_far[k - 1], q_far[k - 1], *state]
        specs += [ANY, ANY, VMEM, VMEM] + [ANY] * (len(state) - 2)
        if not final:
            for i in range(len(state) - 2):
                alias[len(args) - 5 + i] = 4 + i
    size = chunk + LEAD if last else chunk
    tile = (SIDE, HALF)
    outs = [shape((size,) + tile, BF16)] * 2 + [shape((LEAD,) + tile, BF16)] * 2
    sums = [(2 * HALF, 18 * HALF), (2 * HALF, 2 * HALF), (2 * HALF, HALF), (book_rows, HALF), (24, 2 * HALF)]
    scratch = [pltpu.VMEM(dims, F32) for dims in sums]
    out_specs = [ANY] * 4
    if final:
        outs += [shape((layout.half, HALF), F32)] * 2 + [shape((2, layout.half, HALF), BF16)]
        out_specs += [ANY, ANY, VMEM]
    else:
        outs += [shape(dims, F32) for dims in sums]
        out_specs += [ANY] * 5
    scratch += [pltpu.VMEM((18 * HALF, 2 * HALF), BF16)] * 2 + [pltpu.SemaphoreType.DMA((2,))]
    half = chunk // 2
    spots = block * SIDE
    scratch += [
        pltpu.VMEM((LEAD + chunk + 2 * SIDE,) + tile, BF16),
        pltpu.VMEM((LEAD + chunk + 2 * SIDE,) + tile, BF16),
        pltpu.VMEM((LEAD + half,) + tile, F32),
        pltpu.VMEM((LEAD + half,) + tile, BF16),
        pltpu.VMEM((LEAD + chunk + SIDE,) + tile, F32),
        pltpu.VMEM((rows + 2 * block + SIDE,) + tile, BF16),
        pltpu.VMEM((rows + 2 * block + SIDE,) + tile, BF16),
        pltpu.VMEM((rows + 2 * SIDE,) + tile, F32),
        pltpu.VMEM((-(-(rows * SIDE // HALF + 4) // 8) * 8, HALF), jnp.int32),
        pltpu.VMEM(((rows + 2 * block + 2) * SIDE, 6 * HALF), BF16),
        pltpu.VMEM(((rows + 2 * block) * SIDE, 2 * HALF), F32),
        pltpu.VMEM(((rows + 2) * SIDE, 6 * HALF), BF16),
        pltpu.VMEM((rows * SIDE, 2 * HALF), F32),
        pltpu.VMEM((spots, 2 * HALF), BF16),
        pltpu.VMEM((spots, 2 * HALF), F32),
        pltpu.VMEM((spots, 2 * HALF), BF16),
        pltpu.VMEM((spots, 2 * HALF), BF16),
        pltpu.VMEM((spots // 2, HALF), BF16),
        pltpu.VMEM((book_rows, spots), BF16),
        pltpu.VMEM((spots, HALF), BF16),
        pltpu.VMEM((spots, HALF), BF16),
        pltpu.SemaphoreType.DMA((13,)),
    ]
    spots = chunk * SIDE
    return pl.pallas_call(
        functools.partial(main_step, plan, layout, k, len(waits)),
        out_shape=outs,
        in_specs=specs,
        out_specs=out_specs,
        scratch_shapes=scratch,
        input_output_aliases=alias,
        compiler_params=params(58),
        cost_estimate=cost(60 * 65536 * spots, 8 * MIB, 2 * 256 * spots),
        name=f"main_{k}",
    )(*args)


def local(
    image_latents,
    image_heights,
    code_index,
    kernel_three,
    bias_three,
    weight_mix,
    bias_mix,
    weight_project,
    bias_project,
    codebook,
    weight_decode,
    bias_decode,
    out_grad,
):
    images = image_latents.shape[0]
    plan = Plan(images)
    n = len(plan.chunks)
    tile = (SIDE, HALF)
    where = lax.axis_index("mp").astype(jnp.int32)
    core = lax.rem(lax.axis_index("dp").astype(jnp.int32), 2)
    spot = place = jnp.stack([where, core])

    devices = lax.axis_size("dp")
    across = [(i, i ^ 1) for i in range(devices)]
    kernel_half = lax.dynamic_slice_in_dim(kernel_three, core * HALF, HALF, 1)
    far_kernel = trade(kernel_half)
    far_kernel_other = lax.ppermute(far_kernel, "dp", across)

    packed = pl.pallas_call(
        functools.partial(pack_latents, plan),
        out_shape=[
            shape((meta_size(plan),), jnp.int32),
            shape((LEAD + plan.total,) + tile, BF16),
        ]
        + [shape((c,) + tile, BF16) for c in plan.chunks],
        in_specs=[SMEM, SMEM, HBM, ANY],
        out_specs=[SMEM, ANY] + [ANY] * n,
        scratch_shapes=[
            pltpu.VMEM((images, SIDE) + tile, BF16),
            pltpu.VMEM((plan.packed + SIDE,) + tile, BF16),
            pltpu.SemaphoreType.DMA((8,)),
            pltpu.SemaphoreType.DMA((n + 1,)),
        ],
        compiler_params=params(60),
        cost_estimate=cost(0, 12 * MIB),
        name="pack_latents",
    )(image_heights, place, image_latents, kernel_half)
    meta, x_own, x_send = packed[0], packed[1], packed[2:]

    packed = pl.pallas_call(
        functools.partial(pack_code_grads, plan),
        out_shape=[shape((plan.total // 2,) + tile, F32), shape((2 * HALF + HALF // 2 + SIDE, HALF), BF16)]
        + [shape((c // 2,) + tile, BF16) for c in plan.chunks],
        in_specs=[SMEM] + [HBM] * 6 + [ANY],
        out_specs=[VMEM] * (n + 2),
        scratch_shapes=[
            pltpu.VMEM((images, SIDE) + tile, BF16),
            pltpu.VMEM((plan.packed + SIDE,) + tile, BF16),
            pltpu.SemaphoreType.DMA((8,)),
            pltpu.SemaphoreType.DMA((5,)),
            pltpu.VMEM(weight_decode.shape, BF16),
            pltpu.VMEM(weight_mix.shape, BF16),
            pltpu.VMEM(weight_project.shape[::-1], BF16),
            pltpu.VMEM((1, HALF), BF16),
            pltpu.VMEM((1, HALF), BF16),
        ],
        compiler_params=params(60),
        cost_estimate=cost(2 * 2 * plan.total * SIDE * 256 * 128, 10 * MIB),
        name="pack_code_grads",
    )(meta, out_grad, weight_decode, weight_mix, weight_project.T, bias_three.reshape(1, HALF), bias_mix.reshape(1, HALF), far_kernel)
    q_own, small, q_send = packed[0], packed[1], packed[2:]

    book_rows, embed = codebook.shape
    codebook_t = codebook.T
    far_small = trade(small)
    usual = plan.usual
    x_far, q_far = [], []
    x_far.append(trade(x_send[0]))
    q_far.append(trade(q_send[0]))

    weights = pl.pallas_call(
        prepare_weights,
        out_shape=[
            shape((18 * HALF, 2 * HALF), BF16),
            shape((18 * HALF, 2 * HALF), BF16),
            shape((2 * HALF, 2 * HALF), BF16),
            shape((2, 2 * HALF, HALF), BF16),
            shape((SIDE, 2 * HALF), F32),
            shape((HALF, book_rows), BF16),
        ],
        in_specs=[SMEM, HBM, HBM, HBM] + [VMEM] * 4,
        out_specs=[VMEM] * 6,
        scratch_shapes=[pltpu.VMEM(kernel_three.shape, BF16)] * 2 + [pltpu.SemaphoreType.DMA((3,))],
        compiler_params=params(20),
        cost_estimate=cost(0, 5 * MIB),
        name="prepare_weights",
    )(place, kernel_three, far_kernel, far_kernel_other, small, far_small, bias_project.reshape(1, -1), codebook_t)

    groups = 8
    group = images // groups
    codes = code_index.reshape(images, SIDE * SIDE)
    whole = lambda dims: pl.BlockSpec(dims, lambda g: (0,) * len(dims))
    four = pl.BlockSpec((group, SIDE) + tile, lambda g: (g, 0, 0, 0))
    row = pl.BlockSpec((group, SIDE * SIDE), lambda g: (g, 0))
    def code_sums(first, steps):
        return pl.pallas_call(
            functools.partial(sum_codes, first, group),
            grid=(steps,),
            out_shape=shape((embed + 8, HALF), F32),
            in_specs=[
                SMEM,
                pl.BlockSpec((group, SIDE * SIDE), lambda g: (g + first, 0)),
                pl.BlockSpec((group, SIDE) + tile, lambda g: (g + first, 0, 0, 0)),
                whole((embed, book_rows)),
                ANY,
                ANY,
            ],
            out_specs=whole((embed + 8, HALF)),
            scratch_shapes=[
                pltpu.VMEM((book_rows, group * SIDE * SIDE), BF16),
                pltpu.VMEM((group * SIDE * SIDE, HALF), BF16),
                pltpu.VMEM((book_rows, HALF), F32),
            ],
            compiler_params=params(60),
            cost_estimate=cost(steps * group * 256 * 512 * 256, steps * group * 65536),
            name=f"sum_codes_{first}",
        )(image_heights, codes, out_grad, codebook_t, small, far_kernel)

    def decode(after):
        return pl.pallas_call(
            functools.partial(decode_images, plan, groups),
            grid=(groups,),
            out_shape=[shape((images, SIDE) + tile, BF16), shape((8, HALF), F32)],
            in_specs=[SMEM, row, whole((embed, book_rows)), whole((embed, HALF)), whole((1, HALF)), ANY],
            out_specs=[four, whole((8, HALF))],
            scratch_shapes=[pltpu.VMEM((HALF, book_rows), BF16)],
            compiler_params=params(32),
            cost_estimate=cost(images * 256 * 512 * 256, 5 * MIB),
            name="decode_images",
        )(image_heights, codes, codebook_t, weight_decode, bias_decode.reshape(1, HALF), after)

    decode_acc = code_sums(0, groups)
    for k in range(1, usual):
        x_far.append(trade(held(x_send[k], decode_acc, far_small, x_far[0], q_far[0])))
        q_far.append(trade(held(q_send[k], decode_acc, far_small, x_far[0], q_far[0])))

    layout = Layout(devices, book_rows, embed)
    half, piece, chips = layout.half, layout.piece, devices // 2
    streams = (x_own, x_far, q_own, q_far, codes)
    state = None
    win_own, win_far = [], []
    for k in range(usual):
        waits = win_far[k - 2 : k - 1] if k > 1 else []
        ending = (spot, decode_acc) if k == usual - 1 else ()
        outs = run_main(plan, layout, k, meta, image_heights, streams, weights, state, waits, ending)
        win_own.append(outs[0])
        if k < usual - 1:
            win_far.append(trade(outs[1]))
        state = outs[2:]
    last_window = outs[1]
    carry, (keep_own, keep_far, send) = state[:2], state[2:]

    def restore(own, far, waits=()):
        count = len(own)
        return pl.pallas_call(
            functools.partial(restore_rows, plan, count, len(waits)),
            out_shape=[shape((images, SIDE) + tile, BF16), shape((8, HALF), F32)],
            in_specs=[ANY] * len(waits) + [SMEM, SMEM] + [ANY] * (2 * count),
            out_specs=[VMEM, VMEM],
            scratch_shapes=[
                pltpu.VMEM((plan.total + LEAD + SIDE,) + tile, BF16),
                pltpu.VMEM((plan.total + LEAD + SIDE,) + tile, BF16),
                pltpu.SemaphoreType.DMA((2, count)),
            ],
            compiler_params=params(60),
            cost_estimate=cost(0, 10 * MIB),
            name="restore_rows",
        )(*waits, meta, image_heights, *own, *far)


    def step(body, out, name, *args, waits=()):
        specs = [VMEM] * len(args) + [ANY] * len(waits)
        args = (*args, *waits)
        return pl.pallas_call(
            body,
            out_shape=out,
            in_specs=specs,
            out_specs=[VMEM] * len(out) if isinstance(out, list) else VMEM,
            compiler_params=params(24),
            cost_estimate=cost(0, 2 * MIB),
            name=name,
        )(*args)

    send = held(send, win_far[usual - 2])
    came = lax.ppermute(send, "dp", across)
    win_far.append(trade(last_window))
    far_sums = step(add_far, shape((half, HALF), BF16), "add_far", keep_far, came)
    came_far = trade(far_sums)
    parts = [shape((chips, piece, HALF), BF16), shape((8, HALF), F32)]
    mine, token = step(add_own, parts, "add_own", keep_own, came, came_far)
    decoded, token = decode(token)
    cores = [[i for i in range(devices) if i % 2 == c] for c in range(2)]
    mine = lax.all_to_all(mine, "dp", 0, 0, axis_index_groups=cores, tiled=True)
    mine, token = step(add_pieces, parts, "add_pieces", mine, waits=[token])
    latents_grad, token = restore(win_own, win_far, [token])
    mine = lax.all_to_all(mine, "dp", 0, 0, axis_index_groups=cores, tiled=True)
    mine = held(mine, token).reshape(half, HALF)
    theirs = lax.ppermute(mine, "dp", across)

    grads_out = [
        shape((9, 2 * HALF, HALF), F32),
        shape((1, HALF), F32),
        shape((HALF, 2 * HALF), F32),
        shape((1, HALF), F32),
        shape((embed, HALF), F32),
        shape((1, embed), F32),
        shape((embed, book_rows), F32),
        shape((embed, HALF), F32),
        shape((1, HALF), F32),
    ]
    whole = pltpu.VMEM((layout.rows, HALF), F32)

    def usual_end(latents_grad):
        grads = pl.pallas_call(
            functools.partial(write_grads, layout),
            out_shape=grads_out,
            in_specs=[SMEM, VMEM, VMEM],
            out_specs=[VMEM] * 9,
            scratch_shapes=[whole],
            compiler_params=params(24),
            cost_estimate=cost(0, 4 * MIB),
            name="write_grads",
        )(spot, mine, theirs)
        return (latents_grad, *grads)

    def longer_end(latents_grad):
        last_x, last_q = trade(x_send[usual]), trade(q_send[usual])
        streams = (x_own, x_far + [last_x], q_own, q_far + [last_q], codes)
        outs = run_main(plan, layout, usual, meta, image_heights, streams, weights, carry)
        latents_grad, _ = restore(win_own + [outs[0]], win_far + [trade(outs[1])])
        own, far = pl.pallas_call(
            functools.partial(gather_plain, layout),
            out_shape=[shape((layout.rows, HALF), F32)] * 2,
            in_specs=[SMEM] + [VMEM] * 5,
            out_specs=[VMEM] * 2,
            compiler_params=params(40),
            name="gather_plain",
        )(spot, *outs[4:])
        extra = lax.psum(own + trade(far), "dp")
        first, second = jnp.where(core == 0, mine, theirs), jnp.where(core == 0, theirs, mine)
        grads = pl.pallas_call(
            functools.partial(split_again, layout),
            out_shape=grads_out,
            in_specs=[VMEM, VMEM],
            out_specs=[VMEM] * 9,
            scratch_shapes=[whole],
            compiler_params=params(24),
            name="split_again",
        )(jnp.concatenate([first, second]), extra)
        return (latents_grad, *grads)

    flag = layout.bias + 3
    holder = flag // half
    flags = jnp.where(core == holder, mine[flag - holder * half, 0], theirs[flag - holder * half, 0])
    ends = lax.cond(flags.astype(F32) > 0.5, longer_end, usual_end, latents_grad)
    latents_grad, kernel_grad, first_bias, mix_grad, mix_bias, project_grad, project_bias, book, decode, decode_bias = ends
    return (
        decoded,
        latents_grad,
        kernel_grad,
        first_bias.reshape(HALF),
        mix_grad,
        mix_bias.reshape(HALF),
        project_grad.T,
        project_bias.reshape(embed),
        book.T,
        decode,
        decode_bias.reshape(HALF),
    )


def solution(mesh):
    tile = P("dp", None, None, "mp")
    placed = (
        tile,
        P("dp"),
        P("dp", None, None),
        P(None, None, "mp"),
        P("mp"),
        P("mp", None),
        P("mp"),
        P("mp", None),
        P(),
        P(),
        P(None, "mp"),
        P("mp"),
        tile,
    )
    outs = (
        tile,
        tile,
        P(None, None, "mp"),
        P("mp"),
        P("mp", None),
        P("mp"),
        P("mp", None),
        P(),
        P(),
        P(None, "mp"),
        P("mp"),
    )
    return jax.shard_map(local, mesh=mesh, in_specs=placed, out_specs=outs, check_vma=False)
```

profile of v0, /device:TPU:0, one launch (start us, length us, event | category | flops | bytes accessed | tf_op | source)
XLA Modules:
  0.0 173.4 jit_solution(16163161541089400215)
XLA Ops:
  7.2 1.0 constant_dynamic-slice_fusion._
  8.2 0.0 copy-start.29
  8.2 3.0 %collective-permute-start.4 = (bf16[9,128,128]{2,1,0:T(8,128)(2,1)S(1)}, bf16[9,128,128]{2,1,0:T(8,128)(2,1)S(1)}, u32[]{:S(2)}, u32[]{:S(2)}) collective-permute-start(bf16[9,128,128]{2,1,0:T(8,128)(2,1)S(1)} %constant_dynamic-slice_fusion._), channel_id=1, source_target_pairs={{0,1},{1,0},{2,3},{3,2},{4,5},{5,4},{6,7},{7,6},{8,9},{9,8},{10,11... | collective-permute-start | bytes 884744 | tf_op jit(solution)/shard_map/ppermute | solution.py:828
  11.2 0.1 pad_add_fusion.place.refs_0_
  11.3 5.7 %pack_latents.1 = (s32[73]{0:T(128)S(1)}, bf16[536,16,128]{2,1,0:T(8,128)(2,1)}, bf16[152,16,128]{2,1,0:T(8,128)(2,1)}, bf16[224,16,128]{2,1,0:T(8,128)(2,1)}, bf16[144,16,128]{2,1,0:T(8,128)(2,1)}) custom-call(s32[64]{0:T(128)} %refs_2_.1, s32[2]{0:T(128)S(1)} %pad_add_fusion.place.refs_0_, bf16[64,16,16,128]{3,2,1,0:T(8,128)(2,1)} %x_hbm.1, ...), custom_call_target="tpu_custom_call" | custom-call | bytes 12582912 | tf_op jit(solution)/shard_map/pack_latents/pallas_call | solution.py:941
  17.0 0.6 collective-permute-start.6
  17.6 0.6 collective-permute-done.4.rest_5_.__.far_hbm
  18.2 0.7 copy-done.3
  18.9 5.8 %pack_code_grads.1 = (f32[260,16,128]{2,1,0:T(8,128)}, bf16[336,128]{1,0:T(8,128)(2,1)}, bf16[76,16,128]{2,1,0:T(8,128)(2,1)}, bf16[112,16,128]{2,1,0:T(8,128)(2,1)}, bf16[72,16,128]{2,1,0:T(8,128)(2,1)}) custom-call(s32[73]{0:T(128)S(1)} %get-tuple-element.176.meta.refs_0_.refs_2_.refs_1_, bf16[64,16,16,128]{3,2,1,0:T(8,128)(2,1)} %og.1, ...), custom_call_target="tpu_custom_call" | custom-call | flops 1090519040 | bytes 10485760 | tf_op jit(solution)/shard_map/pack_code_grads/pallas_call | solution.py:962
  24.7 1.8 %collective-permute-start.7 = (bf16[76,16,128]{2,1,0:T(8,128)(2,1)}, bf16[76,16,128]{2,1,0:T(8,128)(2,1)S(1)}, u32[]{:S(2)}, u32[]{:S(2)}) collective-permute-start(bf16[76,16,128]{2,1,0:T(8,128)(2,1)} %get-tuple-element.181), channel_id=1, source_target_pairs={{0,1},{1,0},{2,3},{3,2},{4,5},{5,4},{6,7},{7,6},{8,9},{9,8},{10,11... | collective-permute-start | bytes 933896 | tf_op jit(solution)/shard_map/ppermute | solution.py:828
  26.5 0.7 copy.32.codes.refs_6_.refs_8_
  27.2 0.3 collective-permute-start.5
  27.5 9.1 %sum_codes_0.1.refs_1_ = f32[72,128]{1,0:T(8,128)} custom-call(s32[64]{0:T(128)S(1)} %copy-done.32, s32[64,256]{1,0:T(8,128)} %copy.32.codes.refs_6_.refs_8_, bf16[64,16,16,128]{3,2,1,0:T(8,128)(2,1)} %og.1, bf16[64,512]{1,0:T(8,128)(2,1)} %bitcast.18, bf16[336,128]{1,0:T(8,128)(2,1)} %get-tuple-element.177._.small, bf16[9,128,128]{2,1,0:T(8,128)(2,1)} %copy-done.3), custom_call_target="tpu_custom_call" | custom-call | flops 2147483648 | bytes 4194304 | tf_op jit(solution)/shard_map/sum_codes_0/pallas_call | solution.py:1018
  36.6 0.0 copy-start.13
  36.7 4.6 %collective-permute-done.5.refs_2_.far_small = bf16[336,128]{1,0:T(8,128)(2,1)S(1)} collective-permute-done((bf16[336,128]{1,0:T(8,128)(2,1)}, bf16[336,128]{1,0:T(8,128)(2,1)S(1)}, u32[]{:S(2)}, u32[]{:S(2)}) %collective-permute-start.5) | collective-permute-done | bytes 86048 | tf_op jit(solution)/shard_map/ppermute | solution.py:828
  41.3 0.6 copy-done.7
  41.9 0.1 copy-done.28
  42.0 0.2 copy-done.25
  42.3 0.8 collective-permute-start.8
  43.1 0.0 copy-start.8
  43.2 0.9 copy-done.8
  44.0 2.6 %prepare_weights.1 = (bf16[2304,256]{1,0:T(8,128)(2,1)}, bf16[2304,256]{1,0:T(8,128)(2,1)}, bf16[256,256]{1,0:T(8,128)(2,1)S(1)}, bf16[2,256,128]{2,1,0:T(8,128)...) custom-call(s32[2]{0:T(128)S(1)} %pad_add_fusion.place.refs_0_, bf16[9,256,128]{2,1,0:T(8,128)(2,1)S(1)} %copy-done.2, ...), custom_call_target="tpu_custom_call" | custom-call | bytes 5242880 | tf_op jit(solution)/shard_map/prepare_weights/pallas_call | solution.py:993
  46.8 1.3 collective-permute-start.9
  48.0 0.1 copy-done.35
  48.1 25.5 %main_0.1 = (bf16[152,16,128]{2,1,0:T(8,128)(2,1)}, bf16[152,16,128]{2,1,0:T(8,128)(2,1)}, bf16[16,16,128]{2,1,0:T(8,128)(2,1)}, bf16[16,16,128]{2,1,0:T(8,128)(...) custom-call(s32[73]{0:T(128)S(1)} %get-tuple-element.176.meta.refs_0, ...), custom_call_target="tpu_custom_call" | custom-call | flops 9563013120 | bytes 8388608 | tf_op jit(solution)/shard_map/main_0/pallas_call | solution.py:899
  73.6 1.3 collective-permute-start.11
  75.0 37.8 %main_1.1 = (bf16[240,16,128]{2,1,0:T(8,128)(2,1)S(1)}, bf16[240,16,128]{2,1,0:T(8,128)(2,1)}, bf16[16,16,128]{2,1,0:T(8,128)(2,1)S(1)}, bf16[16,16,128]{2,1,0:T...) custom-call(s32[2]{0:T(128)S(1)} %pad_add_fusion.place.refs_0_, ...), custom_call_target="tpu_custom_call" | custom-call | flops 14092861440 | bytes 8388608 | tf_op jit(solution)/shard_map/main_1/pallas_call | solution.py:899
  112.9 0.1 collective-permute-start.12
  113.0 2.5 %collective-permute-done.12.came = bf16[2,1536,128]{2,1,0:T(8,128)(2,1)S(1)} collective-permute-done((bf16[2,1536,128]{2,1,0:T(8,128)(2,1)}, bf16[2,1536,128]{2,1,0:T(8,128)(2,1)S(1)}, u32[]{:S(2)}, u32[]{:S(2)}) %collective-permute-start.12) | collective-permute-done | bytes 786464 | tf_op jit(solution)/shard_map/ppermute | solution.py:1107
  115.4 0.1 add_far.1
  115.6 0.9 collective-permute-start.13
  116.5 10.3 %collective-permute-done.13.came_far = bf16[1536,128]{1,0:T(8,128)(2,1)S(1)} collective-permute-done((bf16[1536,128]{1,0:T(8,128)(2,1)S(1)}, bf16[1536,128]{1,0:T(8,128)(2,1)S(1)}, u32[]{:S(2)}, u32[]{:S(2)}) %collective-permute-start.13) | collective-permute-done | bytes 393248 | tf_op jit(solution)/shard_map/ppermute | solution.py:828
  126.8 0.9 add_own.1
  127.7 4.2 %all-to-all-start = ((bf16[8,192,128]{2,1,0:T(8,128)(2,1)}), bf16[8,192,128]{2,1,0:T(8,128)(2,1)S(1)}, u32[]{:S(2)}, u32[]{:S(2)}) async-start(bf16[8,192,128]{2,1,0:T(8,128)(2,1)} %get-tuple-element.203), calls=%async_computation | async-start | bytes 786432 | tf_op jit(solution)/shard_map/all_to_all | solution.py:1115
  131.9 1.7 %collective-permute-start.14 = (bf16[240,16,128]{2,1,0:T(8,128)(2,1)}, bf16[240,16,128]{2,1,0:T(8,128)(2,1)}, u32[]{:S(2)}, u32[]{:S(2)}) collective-permute-start(bf16[240,16,128]{2,1,0:T(8,128)(2,1)} %get-tuple-element.209), channel_id=1, source_target_pairs={{0,1},{1,0},{2,3},{3,2},{4,5},{5,4},{6,7},{7,6},{8,9},{9,8},{10,11... | collective-permute-start | bytes 2949128 | tf_op jit(solution)/shard_map/ppermute | solution.py:828
  133.7 6.7 %decode_images.1 = (bf16[64,16,16,128]{3,2,1,0:T(8,128)(2,1)}, f32[8,128]{1,0:T(8,128)S(1)}) custom-call(s32[64]{0:T(128)S(1)} %copy-done.32, s32[64,256]{1,0:T(8,128)S(1)} %copy-done.14, bf16[64,512]{1,0:T(8,128)(2,1)S(1)} %bitcast.20, bf16[64,128]{1,0:T(8,128)(2,1)S(1)} %copy-done.16, bf16[1,128]{1,0:T(2,128)(2,1)S(1)} %bitcast.22, ...), custom_call_target="tpu_custom_call" | custom-call | flops 2147483648 | bytes 5242880 | tf_op jit(solution)/shard_map/decode_images/pallas_call | solution.py:1042
  140.4 3.1 %all-to-all-done.pieces = bf16[8,192,128]{2,1,0:T(8,128)(2,1)S(1)} async-done(((bf16[8,192,128]{2,1,0:T(8,128)(2,1)}), bf16[8,192,128]{2,1,0:T(8,128)(2,1)S(1)}, u32[]{:S(2)}, u32[]{:S(2)}) %all-to-all-start) | async-done | bytes 393248 | tf_op jit(solution)/shard_map/all_to_all | solution.py:1115
  143.4 0.8 add_pieces.1
  144.2 0.6 copy-done.17
  144.8 3.6 %all-to-all-start.1 = ((bf16[8,192,128]{2,1,0:T(8,128)(2,1)}), bf16[8,192,128]{2,1,0:T(8,128)(2,1)S(1)}, u32[]{:S(2)}, u32[]{:S(2)}) async-start(bf16[8,192,128]{2,1,0:T(8,128)(2,1)} %get-tuple-element.205), calls=%async_computation.1 | async-start | bytes 786432 | tf_op jit(solution)/shard_map/all_to_all | solution.py:1118
  148.5 6.8 %collective-permute-done.14.refs_6_ = bf16[240,16,128]{2,1,0:T(8,128)(2,1)} collective-permute-done((bf16[240,16,128]{2,1,0:T(8,128)(2,1)}, bf16[240,16,128]{2,1,0:T(8,128)(2,1)}, u32[]{:S(2)}, u32[]{:S(2)}) %collective-permute-start.14) | collective-permute-done | bytes 983072 | tf_op jit(solution)/shard_map/ppermute | solution.py:828
  155.2 5.8 %restore_rows.3 = (bf16[64,16,16,128]{3,2,1,0:T(8,128)(2,1)}, f32[8,128]{1,0:T(8,128)}) custom-call(f32[8,128]{1,0:T(8,128)} %copy-done.17, s32[73]{0:T(128)S(1)} %get-tuple-element.176.meta.refs_0_.refs_2_.refs_1_, s32[64]{0:T(128)S(1)} %copy-done.32, bf16[152,16,128]{2,1,0:T(8,128)(2,1)} %get-tuple-element.207.refs_3_, ...), custom_call_target="tpu_custom_call" | custom-call | bytes 10485760 | tf_op jit(solution)/shard_map/restore_rows/pallas_call | solution.py:1077
  161.0 0.1 collective-permute-start.15
  161.1 0.5 slice.8
  161.6 1.2 collective-permute-done.15
  162.8 0.5 slice.9
  164.7 1.8 %conditional.1 = (bf16[64,16,16,128]{3,2,1,0:T(8,128)(2,1)}, f32[9,256,128]{2,1,0:T(8,128)}, f32[1,128]{1,0:T(1,128)}, f32[128,256]{1,0:T(8,128)}, f32[1,128]{1,...) conditional(s32[]{:T(128)} %convert_element_type.7, ...), branch_computations={%region_0.1_spmd, %region_1.3_spmd} | conditional | flops 9062449152 | bytes 85688968 | solution.py:1177
  164.7 1.8 %write_grads.1 = (f32[9,256,128]{2,1,0:T(8,128)}, f32[1,128]{1,0:T(1,128)}, f32[128,256]{1,0:T(8,128)}, f32[1,128]{1,0:T(1,128)}, f32[64,128]{1,0:T(8,128)}, /*i...) custom-call(s32[2]{0:T(128)S(1)} %get-tuple-element.59.place, ...), custom_call_target="tpu_custom_call" | custom-call | bytes 4194304 | tf_op jit(solution)/shard_map/cond/branch_0_fun/write_grads/pallas_call | solution.py:1136
  (62 shorter events, 0.1 us)
Async XLA Ops:
  8.2 3.1 %copy-start.29 = (bf16[9,128,128]{2,1,0:T(8,128)(2,1)}, bf16[9,128,128]{2,1,0:T(8,128)(2,1)S(1)}, u32[]{:S(2)}) copy-start(bf16[9,128,128]{2,1,0:T(8,128)(2,1)S(1)} %constant_dynamic-slice_fusion._) | copy-start | bytes 884740
  8.2 10.0 %collective-permute-start.4 = (bf16[9,128,128]{2,1,0:T(8,128)(2,1)S(1)}, bf16[9,128,128]{2,1,0:T(8,128)(2,1)S(1)}, u32[]{:S(2)}, u32[]{:S(2)}) collective-permute-start(bf16[9,128,128]{2,1,0:T(8,128)(2,1)S(1)} %constant_dynamic-slice_fusion._), channel_id=1, source_target_pairs={{0,1},{1,0},{2,3},{3,2},{4,5},{5,4},{6,7},{7,6},{8,9},{9,8},{10,11... | collective-permute-start | bytes 884744 | tf_op jit(solution)/shard_map/ppermute | solution.py:828
  17.0 24.3 %collective-permute-start.6 = (bf16[152,16,128]{2,1,0:T(8,128)(2,1)}, bf16[152,16,128]{2,1,0:T(8,128)(2,1)S(1)}, u32[]{:S(2)}, u32[]{:S(2)}) collective-permute-start(bf16[152,16,128]{2,1,0:T(8,128)(2,1)} %get-tuple-element.180), channel_id=1, source_target_pairs={{0,1},{1,0},{2,3},{3,2},{4,5},{5,4},{6,7},{7,6},{8,9},{9,8},{10,11... | collective-permute-start | bytes 1867784 | tf_op jit(solution)/shard_map/ppermute | solution.py:828
  18.2 0.7 copy-start.3
  18.9 7.6 %copy-start.30 = (s32[64,16,16]{0,2,1:T(8,128)S(1)}, s32[64,16,16]{0,2,1:T(8,128)}, u32[]{:S(2)}) copy-start(s32[64,16,16]{0,2,1:T(8,128)} %param.17) | copy-start | bytes 196612
  18.9 8.6 %copy-start.32 = (s32[64]{0:T(128)S(1)}, s32[64]{0:T(128)}, u32[]{:S(2)}) copy-start(s32[64]{0:T(128)} %refs_2_.1) | copy-start | bytes 772
  24.7 16.6 %collective-permute-start.7 = (bf16[76,16,128]{2,1,0:T(8,128)(2,1)}, bf16[76,16,128]{2,1,0:T(8,128)(2,1)S(1)}, u32[]{:S(2)}, u32[]{:S(2)}) collective-permute-start(bf16[76,16,128]{2,1,0:T(8,128)(2,1)} %get-tuple-element.181), channel_id=1, source_target_pairs={{0,1},{1,0},{2,3},{3,2},{4,5},{5,4},{6,7},{7,6},{8,9},{9,8},{10,11... | collective-permute-start | bytes 933896 | tf_op jit(solution)/shard_map/ppermute | solution.py:828
  26.5 16.6 %collective-permute-start.10 = (bf16[9,128,128]{2,1,0:T(8,128)(2,1)}, bf16[9,128,128]{2,1,0:T(8,128)(2,1)S(1)}, u32[]{:S(2)}, u32[]{:S(2)}) collective-permute-start(bf16[9,128,128]{2,1,0:T(8,128)(2,1)} %copy-done.3), channel_id=1, source_target_pairs={{0,2},{2,0},{4,6},{6,4},{8,10},{10,8},{12,14},{14,12},{16,18},{18,... | collective-permute-start | bytes 884744 | tf_op jit(solution)/shard_map/ppermute | solution.py:939
  27.2 14.1 %collective-permute-start.5 = (bf16[336,128]{1,0:T(8,128)(2,1)}, bf16[336,128]{1,0:T(8,128)(2,1)S(1)}, u32[]{:S(2)}, u32[]{:S(2)}) collective-permute-start(bf16[336,128]{1,0:T(8,128)(2,1)} %get-tuple-element.177._.small), channel_id=1, source_target_pairs={{0,1},{1,0},{2,3},{3,2},{4,5},{5,4},{6,7},{7,6},{8,9},{9,8},{10,11... | collective-permute-start | bytes 258056 | tf_op jit(solution)/shard_map/ppermute | solution.py:828
  36.6 6.5 %copy-start.2 = (bf16[9,256,128]{2,1,0:T(8,128)(2,1)S(1)}, bf16[9,256,128]{2,1,0:T(8,128)(2,1)}, u32[]{:S(2)}) copy-start(bf16[9,256,128]{2,1,0:T(8,128)(2,1)} %own_hbm.1) | copy-start | bytes 1769476
  36.6 6.5 %copy-start.4 = (bf16[9,128,128]{2,1,0:T(8,128)(2,1)S(1)}, bf16[9,128,128]{2,1,0:T(8,128)(2,1)}, u32[]{:S(2)}) copy-start(bf16[9,128,128]{2,1,0:T(8,128)(2,1)} %copy-done.3) | copy-start | bytes 884740
  36.6 6.5 %copy-start.12 = (bf16[336,128]{1,0:T(8,128)(2,1)S(1)}, bf16[336,128]{1,0:T(8,128)(2,1)}, u32[]{:S(2)}) copy-start(bf16[336,128]{1,0:T(8,128)(2,1)} %get-tuple-element.177._.small) | copy-start | bytes 258052
  36.6 6.5 %copy-start.13 = (bf16[512,64]{0,1:T(8,128)(2,1)S(1)}, bf16[512,64]{0,1:T(8,128)(2,1)}, u32[]{:S(2)}) copy-start(bf16[512,64]{0,1:T(8,128)(2,1)} %param.24) | copy-start | bytes 196612
  36.7 6.5 %copy-start.18 = (bf16[64]{0:T(256)(128)(2,1)S(1)}, bf16[64]{0:T(256)(128)(2,1)}, u32[]{:S(2)}) copy-start(bf16[64]{0:T(256)(128)(2,1)} %param.23) | copy-start | bytes 388
  41.3 0.6 copy-start.7
  41.3 0.7 copy-start.28
  41.3 1.0 copy-start.25
  42.3 32.7 %collective-permute-start.8 = (bf16[224,16,128]{2,1,0:T(8,128)(2,1)}, bf16[224,16,128]{2,1,0:T(8,128)(2,1)}, u32[]{:S(2)}, u32[]{:S(2)}) collective-permute-start(bf16[224,16,128]{2,1,0:T(8,128)(2,1)} %hold.4), channel_id=1, source_target_pairs={{0,1},{1,0},{2,3},{3,2},{4,5},{5,4},{6,7},{7,6},{8,9},{9,8},{10,11... | collective-permute-start | bytes 2752520 | tf_op jit(solution)/shard_map/ppermute | solution.py:828
  43.1 0.9 copy-start.8
  44.0 4.0 %copy-start.33 = (bf16[536,16,128]{2,1,0:T(8,128)(2,1)S(1)}, bf16[536,16,128]{2,1,0:T(8,128)(2,1)}, u32[]{:S(2)}) copy-start(bf16[536,16,128]{2,1,0:T(8,128)(2,1)} %get-tuple-element.178.refs_2_.refs_4_) | copy-start | bytes 6586372
  46.7 28.3 %copy-start.38 = (bf16[256,256]{1,0:T(8,128)(2,1)}, bf16[256,256]{1,0:T(8,128)(2,1)S(1)}, u32[]{:S(2)}) copy-start(bf16[256,256]{1,0:T(8,128)(2,1)S(1)} %get-tuple-element.186.refs_9_.refs_11_) | copy-start | bytes 393220
  46.7 28.3 %copy-start.39 = (bf16[2,256,128]{2,1,0:T(8,128)(2,1)}, bf16[2,256,128]{2,1,0:T(8,128)(2,1)S(1)}, u32[]{:S(2)}) copy-start(bf16[2,256,128]{2,1,0:T(8,128)(2,1)S(1)} %get-tuple-element.187.refs_10_.refs_12_) | copy-start | bytes 393220
  46.7 28.3 %copy-start.40 = (bf16[128,512]{1,0:T(8,128)(2,1)}, bf16[128,512]{1,0:T(8,128)(2,1)S(1)}, u32[]{:S(2)}) copy-start(bf16[128,512]{1,0:T(8,128)(2,1)S(1)} %get-tuple-element.189.refs_12_.refs_14_) | copy-start | bytes 393220
  46.7 28.3 %copy-start.41 = (f32[16,256]{1,0:T(8,128)}, f32[16,256]{1,0:T(8,128)S(1)}, u32[]{:S(2)}) copy-start(f32[16,256]{1,0:T(8,128)S(1)} %get-tuple-element.188.refs_11_.refs_13_) | copy-start | bytes 49156
  46.7 1.4 copy-start.35
  46.8 28.2 %collective-permute-start.9 = (bf16[112,16,128]{2,1,0:T(8,128)(2,1)}, bf16[112,16,128]{2,1,0:T(8,128)(2,1)}, u32[]{:S(2)}, u32[]{:S(2)}) collective-permute-start(bf16[112,16,128]{2,1,0:T(8,128)(2,1)} %hold.5), channel_id=1, source_target_pairs={{0,1},{1,0},{2,3},{3,2},{4,5},{5,4},{6,7},{7,6},{8,9},{9,8},{10,11... | collective-permute-start | bytes 1376264 | tf_op jit(solution)/shard_map/ppermute | solution.py:828
  48.1 26.9 %copy-start.34 = (bf16[536,16,128]{2,1,0:T(8,128)(2,1)S(1)}, bf16[536,16,128]{2,1,0:T(8,128)(2,1)}, u32[]{:S(2)}) copy-start(bf16[536,16,128]{2,1,0:T(8,128)(2,1)} %get-tuple-element.178.refs_2_.refs_4_) | copy-start | bytes 6586372
  73.6 39.2 %collective-permute-start.11 = (bf16[152,16,128]{2,1,0:T(8,128)(2,1)}, bf16[152,16,128]{2,1,0:T(8,128)(2,1)S(1)}, u32[]{:S(2)}, u32[]{:S(2)}) collective-permute-start(bf16[152,16,128]{2,1,0:T(8,128)(2,1)} %get-tuple-element.199), channel_id=1, source_target_pairs={{0,1},{1,0},{2,3},{3,2},{4,5},{5,4},{6,7},{7,6},{8,9},{9,8},{10,11... | collective-permute-start | bytes 1867784 | tf_op jit(solution)/shard_map/ppermute | solution.py:828
  112.8 2.6 %copy-start.6 = (f32[1536,128]{1,0:T(8,128)S(1)}, f32[1536,128]{1,0:T(8,128)}, u32[]{:S(2)}) copy-start(f32[1536,128]{1,0:T(8,128)} %get-tuple-element.200.keep_far) | copy-start | bytes 2359300
  112.9 14.0 %copy-start.5 = (f32[1536,128]{1,0:T(8,128)S(1)}, f32[1536,128]{1,0:T(8,128)}, u32[]{:S(2)}) copy-start(f32[1536,128]{1,0:T(8,128)} %get-tuple-element.197.keep_own) | copy-start | bytes 2359300
  112.9 2.6 %collective-permute-start.12 = (bf16[2,1536,128]{2,1,0:T(8,128)(2,1)}, bf16[2,1536,128]{2,1,0:T(8,128)(2,1)S(1)}, u32[]{:S(2)}, u32[]{:S(2)}) collective-permute-start(bf16[2,1536,128]{2,1,0:T(8,128)(2,1)} %hold.6), channel_id=1, source_target_pairs={{0,2},{2,0},{4,6},{6,4},{8,10},{10,8},{12,14},{14,12},{16,18},{18,... | collective-permute-start | bytes 2359304 | tf_op jit(solution)/shard_map/ppermute | solution.py:1107
  115.6 18.1 %copy-start.14 = (s32[64,256]{1,0:T(8,128)S(1)}, s32[64,256]{1,0:T(8,128)}, u32[]{:S(2)}) copy-start(s32[64,256]{1,0:T(8,128)} %copy.32.codes.refs_6_.refs_8_) | copy-start | bytes 196612
  115.6 18.1 %copy-start.16 = (bf16[64,128]{1,0:T(8,128)(2,1)S(1)}, bf16[64,128]{1,0:T(8,128)(2,1)}, u32[]{:S(2)}) copy-start(bf16[64,128]{1,0:T(8,128)(2,1)} %decode_w.1) | copy-start | bytes 49156
  115.6 18.1 %copy-start.19 = (bf16[128]{0:T(256)(128)(2,1)S(1)}, bf16[128]{0:T(256)(128)(2,1)}, u32[]{:S(2)}) copy-start(bf16[128]{0:T(256)(128)(2,1)} %param.26) | copy-start | bytes 772
  115.6 11.2 %collective-permute-start.13 = (bf16[1536,128]{1,0:T(8,128)(2,1)S(1)}, bf16[1536,128]{1,0:T(8,128)(2,1)S(1)}, u32[]{:S(2)}, u32[]{:S(2)}) collective-permute-start(bf16[1536,128]{1,0:T(8,128)(2,1)S(1)} %add_far.1), channel_id=1, source_target_pairs={{0,1},{1,0},{2,3},{3,2},{4,5},{5,4},{6,7},{7,6},{8,9},{9,8},{10,11... | collective-permute-start | bytes 1179656 | tf_op jit(solution)/shard_map/ppermute | solution.py:828
  127.7 15.7 %all-to-all-start = ((bf16[8,192,128]{2,1,0:T(8,128)(2,1)}), bf16[8,192,128]{2,1,0:T(8,128)(2,1)S(1)}, u32[]{:S(2)}, u32[]{:S(2)}) async-start(bf16[8,192,128]{2,1,0:T(8,128)(2,1)} %get-tuple-element.203), calls=%async_computation | async-start | bytes 786432 | tf_op jit(solution)/shard_map/all_to_all | solution.py:1115
  131.9 23.3 %collective-permute-start.14 = (bf16[240,16,128]{2,1,0:T(8,128)(2,1)}, bf16[240,16,128]{2,1,0:T(8,128)(2,1)}, u32[]{:S(2)}, u32[]{:S(2)}) collective-permute-start(bf16[240,16,128]{2,1,0:T(8,128)(2,1)} %get-tuple-element.209), channel_id=1, source_target_pairs={{0,1},{1,0},{2,3},{3,2},{4,5},{5,4},{6,7},{7,6},{8,9},{9,8},{10,11... | collective-permute-start | bytes 2949128 | tf_op jit(solution)/shard_map/ppermute | solution.py:828
  144.2 0.6 copy-start.17
  144.8 16.2 %all-to-all-start.1 = ((bf16[8,192,128]{2,1,0:T(8,128)(2,1)}), bf16[8,192,128]{2,1,0:T(8,128)(2,1)S(1)}, u32[]{:S(2)}, u32[]{:S(2)}) async-start(bf16[8,192,128]{2,1,0:T(8,128)(2,1)} %get-tuple-element.205), calls=%async_computation.1 | async-start | bytes 786432 | tf_op jit(solution)/shard_map/all_to_all | solution.py:1118
  155.2 9.4 %copy-start.31 = (s32[64,16,16]{0,2,1:T(8,128)S(1)}, s32[64,16,16]{0,2,1:T(8,128)}, u32[]{:S(2)}) copy-start(s32[64,16,16]{0,2,1:T(8,128)} %param.17) | copy-start | bytes 196612
  155.2 9.4 %copy-start.36 = (bf16[144,16,128]{2,1,0:T(8,128)(2,1)S(1)}, bf16[144,16,128]{2,1,0:T(8,128)(2,1)}, u32[]{:S(2)}) copy-start(bf16[144,16,128]{2,1,0:T(8,128)(2,1)} %get-tuple-element.212) | copy-start | bytes 1769476
  155.2 9.4 %copy-start.37 = (bf16[72,16,128]{2,1,0:T(8,128)(2,1)S(1)}, bf16[72,16,128]{2,1,0:T(8,128)(2,1)}, u32[]{:S(2)}) copy-start(bf16[72,16,128]{2,1,0:T(8,128)(2,1)} %get-tuple-element.213) | copy-start | bytes 884740
  155.2 9.4 %copy-start.42 = (f32[16,256]{1,0:T(8,128)S(1)}, f32[16,256]{1,0:T(8,128)}, u32[]{:S(2)}) copy-start(f32[16,256]{1,0:T(8,128)} %copy-done.41) | copy-start | bytes 49156
  161.0 1.8 %collective-permute-start.15 = (bf16[1536,128]{1,0:T(8,128)(2,1)S(1)}, bf16[1536,128]{1,0:T(8,128)(2,1)S(1)}, u32[]{:S(2)}, u32[]{:S(2)}) collective-permute-start(bf16[1536,128]{1,0:T(8,128)(2,1)S(1)} %bitcast.23), channel_id=1, source_target_pairs={{0,2},{2,0},{4,6},{6,4},{8,10},{10,8},{12,14},{14,12},{16,18},{18,... | collective-permute-start | bytes 1179656 | tf_op jit(solution)/shard_map/ppermute | solution.py:1120
where the time goes:
time: 174 us; the launch traced here: 173 us
  Pallas kernels  103 us (59%)
  waiting for transfers between devices  29 us (17%)
  starting transfers between devices  19.8 us (11%)
  between operations  15.7 us (9%)
  local copies, waits for them, and re-layouts  6.11 us (4%)
    pallas_call x2, Pallas kernels, run_main(): pl.pallas_call(functools.partial(main_step, plan, layout, k, len(waits)),...  63.3 us
    ppermute x9, waiting for transfers between devices, trade(): return lax.ppermute(value, 'mp', [(0, 1), (1, 0)])  22.3 us
    ppermute x9, starting transfers between devices, trade(): return lax.ppermute(value, 'mp', [(0, 1), (1, 0)])  11.8 us
    pallas_call x1, Pallas kernels, code_sums(): pl.pallas_call(functools.partial(sum_codes, first, group), grid=(steps,),...  9.12 us
    all_to_all x2, starting transfers between devices, local(): mine = lax.all_to_all(mine, 'dp', 0, 0, axis_index_groups=cores, tiled=True)  7.86 us
    pallas_call x1, Pallas kernels, decode(): pl.pallas_call(functools.partial(decode_images, plan, groups), grid=(grou...  6.7 us
    pallas_call x1, Pallas kernels, local(): pl.pallas_call(functools.partial(pack_code_grads, plan), out_shape=[shape...  5.77 us
    pallas_call x1, Pallas kernels, restore(): pl.pallas_call(functools.partial(restore_rows, plan, count, len(waits)),...  5.76 us
  transfers between devices with their start and end apart: 14, of which 7 were waited for; matrix products, arithmetic and copies ran while one was open for 1% of the time, Pallas kernels for 58%

commit v1 on v0

--- a/solution.py
+++ b/solution.py
@@ -58,7 +58,7 @@
         self.images = images
         longest = images * SIDE // 2 + SIDE // 2
         part = images // 8
-        self.chunks = [19 * part, 28 * part]
+        self.chunks = [18 * part, 29 * part]
         self.usual = len(self.chunks)
         rest = longest - sum(self.chunks)
         self.chunks.append(rest)
@@ -832,7 +832,7 @@
     return pl.pallas_call(
         hold,
         out_shape=shape(value.shape, value.dtype),
-        in_specs=[ANY] * (1 + len(others)),
+        in_specs=[ANY] + [VMEM if other.size <= 1 << 14 else ANY for other in others],
         out_specs=ANY,
         input_output_aliases={0: 0},
         compiler_params=params(60),
@@ -1043,7 +1043,7 @@
             functools.partial(decode_images, plan, groups),
             grid=(groups,),
             out_shape=[shape((images, SIDE) + tile, BF16), shape((8, HALF), F32)],
-            in_specs=[SMEM, row, whole((embed, book_rows)), whole((embed, HALF)), whole((1, HALF)), ANY],
+            in_specs=[SMEM, row, whole((embed, book_rows)), whole((embed, HALF)), whole((1, HALF)), whole((8, HALF))],
             out_specs=[four, whole((8, HALF))],
             scratch_shapes=[pltpu.VMEM((HALF, book_rows), BF16)],
             compiler_params=params(32),
@@ -1077,7 +1077,7 @@
         return pl.pallas_call(
             functools.partial(restore_rows, plan, count, len(waits)),
             out_shape=[shape((images, SIDE) + tile, BF16), shape((8, HALF), F32)],
-            in_specs=[ANY] * len(waits) + [SMEM, SMEM] + [ANY] * (2 * count),
+            in_specs=[VMEM] * len(waits) + [SMEM, SMEM] + [ANY] * (2 * count),
             out_specs=[VMEM, VMEM],
             scratch_shapes=[
                 pltpu.VMEM((plan.total + LEAD + SIDE,) + tile, BF16),
@@ -1091,7 +1091,7 @@
 
 
     def step(body, out, name, *args, waits=()):
-        specs = [VMEM] * len(args) + [ANY] * len(waits)
+        specs = [VMEM] * (len(args) + len(waits))
         args = (*args, *waits)
         return pl.pallas_call(
             body,

time: 174 us -> 174 us (level)
    all_to_all x2, starting transfers between devices: 7.86 us -> 11.1 us  [local(): mine = lax.all_to_all(mine, 'dp', 0, 0, axis_index_groups=cores, tiled=True)]
    pallas_call x2, Pallas kernels: 63.3 us -> 60.1 us  [run_main(): pl.pallas_call(functools.partial(main_step, plan, layout, k, len(waits)),...]
    pallas_call x4, Pallas kernels: 0.01 us -> 2.38 us  [held(): pl.pallas_call(hold, out_shape=shape(value.shape, value.dtype), in_specs=...]
  transfers between devices with their start and end apart: 14 -> 14, of which waited for: 7 -> 7; matrix products, arithmetic and copies ran while one was open for 1% -> 1% of each run, Pallas kernels for 58% -> 57%
where the time goes in v1:
time: 174 us
  Pallas kernels  102 us (59%)
  waiting for transfers between devices  29.6 us (17%)
  starting transfers between devices  21.3 us (12%)
  between operations  15.8 us (9%)
  local copies, waits for them, and re-layouts  5.15 us (3%)
    pallas_call x2, Pallas kernels, run_main(): pl.pallas_call(functools.partial(main_step, plan, layout, k, len(waits)),...  60.1 us
    ppermute x9, waiting for transfers between devices, trade(): return lax.ppermute(value, 'mp', [(0, 1), (1, 0)])  21.8 us
    all_to_all x2, starting transfers between devices, local(): mine = lax.all_to_all(mine, 'dp', 0, 0, axis_index_groups=cores, tiled=True)  11.1 us
    ppermute x9, starting transfers between devices, trade(): return lax.ppermute(value, 'mp', [(0, 1), (1, 0)])  10.2 us
    pallas_call x1, Pallas kernels, code_sums(): pl.pallas_call(functools.partial(sum_codes, first, group), grid=(steps,),...  9.12 us
    pallas_call x1, Pallas kernels, decode(): pl.pallas_call(functools.partial(decode_images, plan, groups), grid=(grou...  6.71 us
    pallas_call x1, Pallas kernels, restore(): pl.pallas_call(functools.partial(restore_rows, plan, count, len(waits)),...  6.01 us
    pallas_call x1, Pallas kernels, local(): pl.pallas_call(functools.partial(pack_code_grads, plan), out_shape=[shape...  5.77 us
  transfers between devices with their start and end apart: 14, of which 7 were waited for; matrix products, arithmetic and copies ran while one was open for 1% of the time, Pallas kernels for 57%

profile of v1, /device:TPU:0, one launch (start us, length us, event | category | flops | bytes accessed | tf_op | source)
XLA Modules:
  0.0 174.1 jit_solution(8999763506989281460)
XLA Ops:
  7.2 1.0 constant_dynamic-slice_fusion._
  8.2 3.0 %collective-permute-start.4 = (bf16[9,128,128]{2,1,0:T(8,128)(2,1)S(1)}, bf16[9,128,128]{2,1,0:T(8,128)(2,1)S(1)}, u32[]{:S(2)}, u32[]{:S(2)}) collective-permute-start(bf16[9,128,128]{2,1,0:T(8,128)(2,1)S(1)} %constant_dynamic-slice_fusion._), channel_id=1, source_target_pairs={{0,1},{1,0},{2,3},{3,2},{4,5},{5,4},{6,7},{7,6},{8,9},{9,8},{10,11... | collective-permute-start | bytes 884744 | tf_op jit(solution)/shard_map/ppermute | solution.py:828
  11.2 0.1 pad_add_fusion.place.refs_0_
  11.3 5.7 %pack_latents.1 = (s32[73]{0:T(128)S(1)}, bf16[536,16,128]{2,1,0:T(8,128)(2,1)}, bf16[144,16,128]{2,1,0:T(8,128)(2,1)}, bf16[232,16,128]{2,1,0:T(8,128)(2,1)}, bf16[144,16,128]{2,1,0:T(8,128)(2,1)}) custom-call(s32[64]{0:T(128)} %refs_2_.1, s32[2]{0:T(128)S(1)} %pad_add_fusion.place.refs_0_, bf16[64,16,16,128]{3,2,1,0:T(8,128)(2,1)} %x_hbm.1, ...), custom_call_target="tpu_custom_call" | custom-call | bytes 12582912 | tf_op jit(solution)/shard_map/pack_latents/pallas_call | solution.py:941
  17.0 0.0 copy-start.36
  17.0 0.6 collective-permute-start.6
  17.6 0.6 collective-permute-done.4.rest_5_.__.far_hbm
  18.2 0.7 copy-done.3
  18.9 5.8 %pack_code_grads.1 = (f32[260,16,128]{2,1,0:T(8,128)}, bf16[336,128]{1,0:T(8,128)(2,1)}, bf16[72,16,128]{2,1,0:T(8,128)(2,1)}, bf16[116,16,128]{2,1,0:T(8,128)(2,1)}, bf16[72,16,128]{2,1,0:T(8,128)(2,1)}) custom-call(s32[73]{0:T(128)S(1)} %get-tuple-element.176.meta.refs_0_.refs_2_.refs_1_, bf16[64,16,16,128]{3,2,1,0:T(8,128)(2,1)} %og.1, ...), custom_call_target="tpu_custom_call" | custom-call | flops 1090519040 | bytes 10485760 | tf_op jit(solution)/shard_map/pack_code_grads/pallas_call | solution.py:962
  24.7 1.8 %collective-permute-start.7 = (bf16[72,16,128]{2,1,0:T(8,128)(2,1)}, bf16[72,16,128]{2,1,0:T(8,128)(2,1)S(1)}, u32[]{:S(2)}, u32[]{:S(2)}) collective-permute-start(bf16[72,16,128]{2,1,0:T(8,128)(2,1)} %get-tuple-element.181), channel_id=1, source_target_pairs={{0,1},{1,0},{2,3},{3,2},{4,5},{5,4},{6,7},{7,6},{8,9},{9,8},{10,11... | collective-permute-start | bytes 884744 | tf_op jit(solution)/shard_map/ppermute | solution.py:828
  26.5 0.7 copy.32.codes.refs_6_.refs_8_
  27.3 0.3 collective-permute-start.5
  27.5 9.1 %sum_codes_0.1.refs_1_ = f32[72,128]{1,0:T(8,128)} custom-call(s32[64]{0:T(128)S(1)} %copy-done.34, s32[64,256]{1,0:T(8,128)} %copy.32.codes.refs_6_.refs_8_, bf16[64,16,16,128]{3,2,1,0:T(8,128)(2,1)} %og.1, bf16[64,512]{1,0:T(8,128)(2,1)} %bitcast.18, bf16[336,128]{1,0:T(8,128)(2,1)} %get-tuple-element.177._.small, bf16[9,128,128]{2,1,0:T(8,128)(2,1)} %copy-done.3), custom_call_target="tpu_custom_call" | custom-call | flops 2147483648 | bytes 4194304 | tf_op jit(solution)/shard_map/sum_codes_0/pallas_call | solution.py:1018
  36.7 3.6 %collective-permute-done.5.refs_2_.far_small = bf16[336,128]{1,0:T(8,128)(2,1)S(1)} collective-permute-done((bf16[336,128]{1,0:T(8,128)(2,1)}, bf16[336,128]{1,0:T(8,128)(2,1)S(1)}, u32[]{:S(2)}, u32[]{:S(2)}) %collective-permute-start.5) | collective-permute-done | bytes 86048 | tf_op jit(solution)/shard_map/ppermute | solution.py:828
  40.3 0.6 copy-done.7
  40.9 0.1 copy-done.29
  41.0 0.2 copy-done.25
  41.2 0.8 hold.4
  42.0 0.0 copy-start.13
  42.0 0.0 copy-start.18
  42.0 0.9 collective-permute-start.8
  42.9 0.9 hold.5
  43.8 1.2 collective-permute-start.9
  45.1 2.6 %prepare_weights.1 = (bf16[2304,256]{1,0:T(8,128)(2,1)}, bf16[2304,256]{1,0:T(8,128)(2,1)}, bf16[256,256]{1,0:T(8,128)(2,1)S(1)}, bf16[2,256,128]{2,1,0:T(8,128)...) custom-call(s32[2]{0:T(128)S(1)} %pad_add_fusion.place.refs_0_, bf16[9,256,128]{2,1,0:T(8,128)(2,1)S(1)} %copy-done.2, ...), custom_call_target="tpu_custom_call" | custom-call | bytes 5242880 | tf_op jit(solution)/shard_map/prepare_weights/pallas_call | solution.py:993
  47.8 25.7 %main_0.1 = (bf16[144,16,128]{2,1,0:T(8,128)(2,1)}, bf16[144,16,128]{2,1,0:T(8,128)(2,1)}, bf16[16,16,128]{2,1,0:T(8,128)(2,1)}, bf16[16,16,128]{2,1,0:T(8,128)(...) custom-call(s32[73]{0:T(128)S(1)} %get-tuple-element.176.meta.refs_0, ...), custom_call_target="tpu_custom_call" | custom-call | flops 9059696640 | bytes 8388608 | tf_op jit(solution)/shard_map/main_0/pallas_call | solution.py:899
  73.5 1.0 collective-permute-start.11
  74.6 34.4 %main_1.1 = (bf16[248,16,128]{2,1,0:T(8,128)(2,1)S(1)}, bf16[248,16,128]{2,1,0:T(8,128)(2,1)}, bf16[16,16,128]{2,1,0:T(8,128)(2,1)S(1)}, bf16[16,16,128]{2,1,0:T...) custom-call(s32[2]{0:T(128)S(1)} %pad_add_fusion.place.refs_0_, ...), custom_call_target="tpu_custom_call" | custom-call | flops 14596177920 | bytes 8388608 | tf_op jit(solution)/shard_map/main_1/pallas_call | solution.py:899
  109.1 0.1 collective-permute-start.12
  109.1 2.5 %collective-permute-done.12.came = bf16[2,1536,128]{2,1,0:T(8,128)(2,1)S(1)} collective-permute-done((bf16[2,1536,128]{2,1,0:T(8,128)(2,1)}, bf16[2,1536,128]{2,1,0:T(8,128)(2,1)S(1)}, u32[]{:S(2)}, u32[]{:S(2)}) %collective-permute-start.12) | collective-permute-done | bytes 786464 | tf_op jit(solution)/shard_map/ppermute | solution.py:1107
  111.6 0.1 add_far.1
  111.8 1.1 collective-permute-start.13
  112.9 10.2 %collective-permute-done.13.came_far = bf16[1536,128]{1,0:T(8,128)(2,1)S(1)} collective-permute-done((bf16[1536,128]{1,0:T(8,128)(2,1)S(1)}, bf16[1536,128]{1,0:T(8,128)(2,1)S(1)}, u32[]{:S(2)}, u32[]{:S(2)}) %collective-permute-start.13) | collective-permute-done | bytes 393248 | tf_op jit(solution)/shard_map/ppermute | solution.py:828
  123.0 0.9 add_own.1
  123.9 7.5 %all-to-all-start = ((bf16[8,192,128]{2,1,0:T(8,128)(2,1)}), bf16[8,192,128]{2,1,0:T(8,128)(2,1)S(1)}, u32[]{:S(2)}, u32[]{:S(2)}) async-start(bf16[8,192,128]{2,1,0:T(8,128)(2,1)} %get-tuple-element.203), calls=%async_computation | async-start | bytes 786432 | tf_op jit(solution)/shard_map/all_to_all | solution.py:1115
  131.4 0.3 collective-permute-start.14
  131.7 6.7 %decode_images.1 = (bf16[64,16,16,128]{3,2,1,0:T(8,128)(2,1)}, f32[8,128]{1,0:T(8,128)S(1)}) custom-call(s32[64]{0:T(128)S(1)} %copy-done.35, s32[64,256]{1,0:T(8,128)S(1)} %copy-done.14, bf16[64,512]{1,0:T(8,128)(2,1)S(1)} %bitcast.20, bf16[64,128]{1,0:T(8,128)(2,1)S(1)} %copy-done.16, bf16[1,128]{1,0:T(2,128)(2,1)S(1)} %bitcast.22, ...), custom_call_target="tpu_custom_call" | custom-call | flops 2147483648 | bytes 5242880 | tf_op jit(solution)/shard_map/decode_images/pallas_call | solution.py:1042
  138.4 4.2 %all-to-all-done.pieces = bf16[8,192,128]{2,1,0:T(8,128)(2,1)S(1)} async-done(((bf16[8,192,128]{2,1,0:T(8,128)(2,1)}), bf16[8,192,128]{2,1,0:T(8,128)(2,1)S(1)}, u32[]{:S(2)}, u32[]{:S(2)}) %all-to-all-start) | async-done | bytes 393248 | tf_op jit(solution)/shard_map/all_to_all | solution.py:1115
  142.6 0.8 add_pieces.1
  143.4 0.6 copy-done.17
  144.0 3.6 %all-to-all-start.1 = ((bf16[8,192,128]{2,1,0:T(8,128)(2,1)}), bf16[8,192,128]{2,1,0:T(8,128)(2,1)S(1)}, u32[]{:S(2)}, u32[]{:S(2)}) async-start(bf16[8,192,128]{2,1,0:T(8,128)(2,1)} %get-tuple-element.205), calls=%async_computation.1 | async-start | bytes 786432 | tf_op jit(solution)/shard_map/all_to_all | solution.py:1118
  147.6 7.5 %collective-permute-done.14.refs_6_ = bf16[248,16,128]{2,1,0:T(8,128)(2,1)} collective-permute-done((bf16[248,16,128]{2,1,0:T(8,128)(2,1)}, bf16[248,16,128]{2,1,0:T(8,128)(2,1)}, u32[]{:S(2)}, u32[]{:S(2)}) %collective-permute-start.14) | collective-permute-done | bytes 1015840 | tf_op jit(solution)/shard_map/ppermute | solution.py:828
  155.1 6.0 %restore_rows.3 = (bf16[64,16,16,128]{3,2,1,0:T(8,128)(2,1)}, f32[8,128]{1,0:T(8,128)}) custom-call(f32[8,128]{1,0:T(8,128)} %copy-done.17, s32[73]{0:T(128)S(1)} %copy-done.37, s32[64]{0:T(128)S(1)} %copy-done.35, bf16[144,16,128]{2,1,0:T(8,128)(2,1)} %get-tuple-element.207.refs_3_, bf16[248,16,128]{2,1,0:T(8,128)(2,1)S(1)} %get-tuple-element.208.refs_4_, ...), custom_call_target="tpu_custom_call" | custom-call | bytes 10485760 | tf_op jit(solution)/shard_map/restore_rows/pallas_call | solution.py:1077
  161.1 0.7 hold.7
  161.8 0.5 slice.8
  162.3 1.2 collective-permute-done.15
  163.5 0.5 slice.9
  165.4 1.8 %conditional.1 = (bf16[64,16,16,128]{3,2,1,0:T(8,128)(2,1)}, f32[9,256,128]{2,1,0:T(8,128)}, f32[1,128]{1,0:T(1,128)}, f32[128,256]{1,0:T(8,128)}, f32[1,128]{1,...) conditional(s32[]{:T(128)} %convert_element_type.7, ...), branch_computations={%region_0.1_spmd, %region_1.3_spmd} | conditional | flops 9062449152 | bytes 85557896 | solution.py:1177
  165.4 1.8 %write_grads.1 = (f32[9,256,128]{2,1,0:T(8,128)}, f32[1,128]{1,0:T(1,128)}, f32[128,256]{1,0:T(8,128)}, f32[1,128]{1,0:T(1,128)}, f32[64,128]{1,0:T(8,128)}, /*i...) custom-call(s32[2]{0:T(128)S(1)} %get-tuple-element.59.place, ...), custom_call_target="tpu_custom_call" | custom-call | bytes 4194304 | tf_op jit(solution)/shard_map/cond/branch_0_fun/write_grads/pallas_call | solution.py:1136
  (72 shorter events, 0.2 us)
Async XLA Ops:
  8.2 3.1 %copy-start.28 = (bf16[9,128,128]{2,1,0:T(8,128)(2,1)}, bf16[9,128,128]{2,1,0:T(8,128)(2,1)S(1)}, u32[]{:S(2)}) copy-start(bf16[9,128,128]{2,1,0:T(8,128)(2,1)S(1)} %constant_dynamic-slice_fusion._) | copy-start | bytes 884740
  8.2 10.0 %collective-permute-start.4 = (bf16[9,128,128]{2,1,0:T(8,128)(2,1)S(1)}, bf16[9,128,128]{2,1,0:T(8,128)(2,1)S(1)}, u32[]{:S(2)}, u32[]{:S(2)}) collective-permute-start(bf16[9,128,128]{2,1,0:T(8,128)(2,1)S(1)} %constant_dynamic-slice_fusion._), channel_id=1, source_target_pairs={{0,1},{1,0},{2,3},{3,2},{4,5},{5,4},{6,7},{7,6},{8,9},{9,8},{10,11... | collective-permute-start | bytes 884744 | tf_op jit(solution)/shard_map/ppermute | solution.py:828
  11.3 63.3 %copy-start.32 = (s32[2]{0:T(128)}, s32[2]{0:T(128)S(1)}, u32[]{:S(2)}) copy-start(s32[2]{0:T(128)S(1)} %pad_add_fusion.place.refs_0_) | copy-start | bytes 28
  17.0 57.5 %copy-start.36 = (s32[73]{0:T(128)}, s32[73]{0:T(128)S(1)}, u32[]{:S(2)}) copy-start(s32[73]{0:T(128)S(1)} %get-tuple-element.176.meta.refs_0_.refs_2_.refs_1_) | copy-start | bytes 880
  17.0 23.2 %collective-permute-start.6 = (bf16[144,16,128]{2,1,0:T(8,128)(2,1)}, bf16[144,16,128]{2,1,0:T(8,128)(2,1)S(1)}, u32[]{:S(2)}, u32[]{:S(2)}) collective-permute-start(bf16[144,16,128]{2,1,0:T(8,128)(2,1)} %get-tuple-element.180), channel_id=1, source_target_pairs={{0,1},{1,0},{2,3},{3,2},{4,5},{5,4},{6,7},{7,6},{8,9},{9,8},{10,11... | collective-permute-start | bytes 1769480 | tf_op jit(solution)/shard_map/ppermute | solution.py:828
  18.2 0.7 copy-start.3
  18.9 7.6 %copy-start.30 = (s32[64,16,16]{0,2,1:T(8,128)S(1)}, s32[64,16,16]{0,2,1:T(8,128)}, u32[]{:S(2)}) copy-start(s32[64,16,16]{0,2,1:T(8,128)} %param.17) | copy-start | bytes 196612
  18.9 8.6 %copy-start.34 = (s32[64]{0:T(128)S(1)}, s32[64]{0:T(128)}, u32[]{:S(2)}) copy-start(s32[64]{0:T(128)} %refs_2_.1) | copy-start | bytes 772
  24.7 15.5 %collective-permute-start.7 = (bf16[72,16,128]{2,1,0:T(8,128)(2,1)}, bf16[72,16,128]{2,1,0:T(8,128)(2,1)S(1)}, u32[]{:S(2)}, u32[]{:S(2)}) collective-permute-start(bf16[72,16,128]{2,1,0:T(8,128)(2,1)} %get-tuple-element.181), channel_id=1, source_target_pairs={{0,1},{1,0},{2,3},{3,2},{4,5},{5,4},{6,7},{7,6},{8,9},{9,8},{10,11... | collective-permute-start | bytes 884744 | tf_op jit(solution)/shard_map/ppermute | solution.py:828
  27.3 13.0 %collective-permute-start.5 = (bf16[336,128]{1,0:T(8,128)(2,1)}, bf16[336,128]{1,0:T(8,128)(2,1)S(1)}, u32[]{:S(2)}, u32[]{:S(2)}) collective-permute-start(bf16[336,128]{1,0:T(8,128)(2,1)} %get-tuple-element.177._.small), channel_id=1, source_target_pairs={{0,1},{1,0},{2,3},{3,2},{4,5},{5,4},{6,7},{7,6},{8,9},{9,8},{10,11... | collective-permute-start | bytes 258056 | tf_op jit(solution)/shard_map/ppermute | solution.py:828
  27.5 17.5 %collective-permute-start.10 = (bf16[9,128,128]{2,1,0:T(8,128)(2,1)}, bf16[9,128,128]{2,1,0:T(8,128)(2,1)S(1)}, u32[]{:S(2)}, u32[]{:S(2)}) collective-permute-start(bf16[9,128,128]{2,1,0:T(8,128)(2,1)} %copy-done.3), channel_id=1, source_target_pairs={{0,2},{2,0},{4,6},{6,4},{8,10},{10,8},{12,14},{14,12},{16,18},{18,... | collective-permute-start | bytes 884744 | tf_op jit(solution)/shard_map/ppermute | solution.py:939
  40.2 0.6 copy-start.7
  40.2 0.7 copy-start.29
  40.3 0.9 copy-start.25
  42.0 3.1 %copy-start.2 = (bf16[9,256,128]{2,1,0:T(8,128)(2,1)S(1)}, bf16[9,256,128]{2,1,0:T(8,128)(2,1)}, u32[]{:S(2)}) copy-start(bf16[9,256,128]{2,1,0:T(8,128)(2,1)} %own_hbm.1) | copy-start | bytes 1769476
  42.0 3.1 %copy-start.4 = (bf16[9,128,128]{2,1,0:T(8,128)(2,1)S(1)}, bf16[9,128,128]{2,1,0:T(8,128)(2,1)}, u32[]{:S(2)}) copy-start(bf16[9,128,128]{2,1,0:T(8,128)(2,1)} %copy-done.3) | copy-start | bytes 884740
  42.0 3.1 %copy-start.8 = (bf16[336,128]{1,0:T(8,128)(2,1)S(1)}, bf16[336,128]{1,0:T(8,128)(2,1)}, u32[]{:S(2)}) copy-start(bf16[336,128]{1,0:T(8,128)(2,1)} %copy-done.7) | copy-start | bytes 258052
  42.0 3.1 %copy-start.12 = (bf16[336,128]{1,0:T(8,128)(2,1)S(1)}, bf16[336,128]{1,0:T(8,128)(2,1)}, u32[]{:S(2)}) copy-start(bf16[336,128]{1,0:T(8,128)(2,1)} %get-tuple-element.177._.small) | copy-start | bytes 258052
  42.0 3.1 %copy-start.13 = (bf16[512,64]{0,1:T(8,128)(2,1)S(1)}, bf16[512,64]{0,1:T(8,128)(2,1)}, u32[]{:S(2)}) copy-start(bf16[512,64]{0,1:T(8,128)(2,1)} %param.24) | copy-start | bytes 196612
  42.0 3.1 %copy-start.18 = (bf16[64]{0:T(256)(128)(2,1)S(1)}, bf16[64]{0:T(256)(128)(2,1)}, u32[]{:S(2)}) copy-start(bf16[64]{0:T(256)(128)(2,1)} %param.23) | copy-start | bytes 388
  42.0 32.5 %collective-permute-start.8 = (bf16[232,16,128]{2,1,0:T(8,128)(2,1)}, bf16[232,16,128]{2,1,0:T(8,128)(2,1)}, u32[]{:S(2)}, u32[]{:S(2)}) collective-permute-start(bf16[232,16,128]{2,1,0:T(8,128)(2,1)} %hold.4), channel_id=1, source_target_pairs={{0,1},{1,0},{2,3},{3,2},{4,5},{5,4},{6,7},{7,6},{8,9},{9,8},{10,11... | collective-permute-start | bytes 2850824 | tf_op jit(solution)/shard_map/ppermute | solution.py:828
  42.9 4.9 %copy-start.38 = (bf16[536,16,128]{2,1,0:T(8,128)(2,1)S(1)}, bf16[536,16,128]{2,1,0:T(8,128)(2,1)}, u32[]{:S(2)}) copy-start(bf16[536,16,128]{2,1,0:T(8,128)(2,1)} %get-tuple-element.178.refs_2_.refs_4_) | copy-start | bytes 6586372
  43.8 30.7 %collective-permute-start.9 = (bf16[116,16,128]{2,1,0:T(8,128)(2,1)}, bf16[116,16,128]{2,1,0:T(8,128)(2,1)}, u32[]{:S(2)}, u32[]{:S(2)}) collective-permute-start(bf16[116,16,128]{2,1,0:T(8,128)(2,1)} %hold.5), channel_id=1, source_target_pairs={{0,1},{1,0},{2,3},{3,2},{4,5},{5,4},{6,7},{7,6},{8,9},{9,8},{10,11... | collective-permute-start | bytes 1425416 | tf_op jit(solution)/shard_map/ppermute | solution.py:828
  47.7 26.8 %copy-start.43 = (bf16[256,256]{1,0:T(8,128)(2,1)}, bf16[256,256]{1,0:T(8,128)(2,1)S(1)}, u32[]{:S(2)}) copy-start(bf16[256,256]{1,0:T(8,128)(2,1)S(1)} %get-tuple-element.186.refs_9_.refs_11_) | copy-start | bytes 393220
  47.7 26.8 %copy-start.44 = (bf16[2,256,128]{2,1,0:T(8,128)(2,1)}, bf16[2,256,128]{2,1,0:T(8,128)(2,1)S(1)}, u32[]{:S(2)}) copy-start(bf16[2,256,128]{2,1,0:T(8,128)(2,1)S(1)} %get-tuple-element.187.refs_10_.refs_12_) | copy-start | bytes 393220
  47.7 26.8 %copy-start.45 = (bf16[128,512]{1,0:T(8,128)(2,1)}, bf16[128,512]{1,0:T(8,128)(2,1)S(1)}, u32[]{:S(2)}) copy-start(bf16[128,512]{1,0:T(8,128)(2,1)S(1)} %get-tuple-element.189.refs_12_.refs_14_) | copy-start | bytes 393220
  47.7 26.8 %copy-start.46 = (f32[16,256]{1,0:T(8,128)}, f32[16,256]{1,0:T(8,128)S(1)}, u32[]{:S(2)}) copy-start(f32[16,256]{1,0:T(8,128)S(1)} %get-tuple-element.188.refs_11_.refs_13_) | copy-start | bytes 49156
  47.8 26.8 %copy-start.39 = (bf16[536,16,128]{2,1,0:T(8,128)(2,1)S(1)}, bf16[536,16,128]{2,1,0:T(8,128)(2,1)}, u32[]{:S(2)}) copy-start(bf16[536,16,128]{2,1,0:T(8,128)(2,1)} %get-tuple-element.178.refs_2_.refs_4_) | copy-start | bytes 6586372
  47.8 26.8 %copy-start.40 = (bf16[2304,256]{1,0:T(8,128)(2,1)S(1)}, bf16[2304,256]{1,0:T(8,128)(2,1)}, u32[]{:S(2)}) copy-start(bf16[2304,256]{1,0:T(8,128)(2,1)} %get-tuple-element.184.refs_7_.refs_9_) | copy-start | bytes 3538948
  73.5 35.5 %collective-permute-start.11 = (bf16[144,16,128]{2,1,0:T(8,128)(2,1)}, bf16[144,16,128]{2,1,0:T(8,128)(2,1)S(1)}, u32[]{:S(2)}, u32[]{:S(2)}) collective-permute-start(bf16[144,16,128]{2,1,0:T(8,128)(2,1)} %get-tuple-element.199), channel_id=1, source_target_pairs={{0,1},{1,0},{2,3},{3,2},{4,5},{5,4},{6,7},{7,6},{8,9},{9,8},{10,11... | collective-permute-start | bytes 1769480 | tf_op jit(solution)/shard_map/ppermute | solution.py:828
  109.0 2.6 %copy-start.6 = (f32[1536,128]{1,0:T(8,128)S(1)}, f32[1536,128]{1,0:T(8,128)}, u32[]{:S(2)}) copy-start(f32[1536,128]{1,0:T(8,128)} %get-tuple-element.200.keep_far) | copy-start | bytes 2359300
  109.0 14.0 %copy-start.5 = (f32[1536,128]{1,0:T(8,128)S(1)}, f32[1536,128]{1,0:T(8,128)}, u32[]{:S(2)}) copy-start(f32[1536,128]{1,0:T(8,128)} %get-tuple-element.197.keep_own) | copy-start | bytes 2359300
  109.1 2.6 %collective-permute-start.12 = (bf16[2,1536,128]{2,1,0:T(8,128)(2,1)}, bf16[2,1536,128]{2,1,0:T(8,128)(2,1)S(1)}, u32[]{:S(2)}, u32[]{:S(2)}) collective-permute-start(bf16[2,1536,128]{2,1,0:T(8,128)(2,1)} %hold.6), channel_id=1, source_target_pairs={{0,2},{2,0},{4,6},{6,4},{8,10},{10,8},{12,14},{14,12},{16,18},{18,... | collective-permute-start | bytes 2359304 | tf_op jit(solution)/shard_map/ppermute | solution.py:1107
  111.7 19.9 %copy-start.14 = (s32[64,256]{1,0:T(8,128)S(1)}, s32[64,256]{1,0:T(8,128)}, u32[]{:S(2)}) copy-start(s32[64,256]{1,0:T(8,128)} %copy.32.codes.refs_6_.refs_8_) | copy-start | bytes 196612
  111.7 19.9 %copy-start.16 = (bf16[64,128]{1,0:T(8,128)(2,1)S(1)}, bf16[64,128]{1,0:T(8,128)(2,1)}, u32[]{:S(2)}) copy-start(bf16[64,128]{1,0:T(8,128)(2,1)} %decode_w.1) | copy-start | bytes 49156
  111.8 19.9 %copy-start.19 = (bf16[128]{0:T(256)(128)(2,1)S(1)}, bf16[128]{0:T(256)(128)(2,1)}, u32[]{:S(2)}) copy-start(bf16[128]{0:T(256)(128)(2,1)} %param.26) | copy-start | bytes 772
  111.8 19.9 %copy-start.35 = (s32[64]{0:T(128)S(1)}, s32[64]{0:T(128)}, u32[]{:S(2)}) copy-start(s32[64]{0:T(128)} %refs_2_.1) | copy-start | bytes 772
  111.8 11.2 %collective-permute-start.13 = (bf16[1536,128]{1,0:T(8,128)(2,1)S(1)}, bf16[1536,128]{1,0:T(8,128)(2,1)S(1)}, u32[]{:S(2)}, u32[]{:S(2)}) collective-permute-start(bf16[1536,128]{1,0:T(8,128)(2,1)S(1)} %add_far.1), channel_id=1, source_target_pairs={{0,1},{1,0},{2,3},{3,2},{4,5},{5,4},{6,7},{7,6},{8,9},{9,8},{10,11... | collective-permute-start | bytes 1179656 | tf_op jit(solution)/shard_map/ppermute | solution.py:828
  123.9 18.7 %all-to-all-start = ((bf16[8,192,128]{2,1,0:T(8,128)(2,1)}), bf16[8,192,128]{2,1,0:T(8,128)(2,1)S(1)}, u32[]{:S(2)}, u32[]{:S(2)}) async-start(bf16[8,192,128]{2,1,0:T(8,128)(2,1)} %get-tuple-element.203), calls=%async_computation | async-start | bytes 786432 | tf_op jit(solution)/shard_map/all_to_all | solution.py:1115
  131.4 23.7 %collective-permute-start.14 = (bf16[248,16,128]{2,1,0:T(8,128)(2,1)}, bf16[248,16,128]{2,1,0:T(8,128)(2,1)}, u32[]{:S(2)}, u32[]{:S(2)}) collective-permute-start(bf16[248,16,128]{2,1,0:T(8,128)(2,1)} %get-tuple-element.209), channel_id=1, source_target_pairs={{0,1},{1,0},{2,3},{3,2},{4,5},{5,4},{6,7},{7,6},{8,9},{9,8},{10,11... | collective-permute-start | bytes 3047432 | tf_op jit(solution)/shard_map/ppermute | solution.py:828
  131.7 23.4 %copy-start.37 = (s32[73]{0:T(128)S(1)}, s32[73]{0:T(128)}, u32[]{:S(2)}) copy-start(s32[73]{0:T(128)} %copy-done.36) | copy-start | bytes 880
  144.0 17.1 %all-to-all-start.1 = ((bf16[8,192,128]{2,1,0:T(8,128)(2,1)}), bf16[8,192,128]{2,1,0:T(8,128)(2,1)S(1)}, u32[]{:S(2)}, u32[]{:S(2)}) async-start(bf16[8,192,128]{2,1,0:T(8,128)(2,1)} %get-tuple-element.205), calls=%async_computation.1 | async-start | bytes 786432 | tf_op jit(solution)/shard_map/all_to_all | solution.py:1118
  155.1 10.3 %copy-start.31 = (s32[64,16,16]{0,2,1:T(8,128)S(1)}, s32[64,16,16]{0,2,1:T(8,128)}, u32[]{:S(2)}) copy-start(s32[64,16,16]{0,2,1:T(8,128)} %param.17) | copy-start | bytes 196612
  155.1 10.3 %copy-start.33 = (s32[2]{0:T(128)S(1)}, s32[2]{0:T(128)}, u32[]{:S(2)}) copy-start(s32[2]{0:T(128)} %copy-done.32) | copy-start | bytes 28
  155.1 10.3 %copy-start.41 = (bf16[144,16,128]{2,1,0:T(8,128)(2,1)S(1)}, bf16[144,16,128]{2,1,0:T(8,128)(2,1)}, u32[]{:S(2)}) copy-start(bf16[144,16,128]{2,1,0:T(8,128)(2,1)} %get-tuple-element.212) | copy-start | bytes 1769476
  155.1 10.3 %copy-start.42 = (bf16[72,16,128]{2,1,0:T(8,128)(2,1)S(1)}, bf16[72,16,128]{2,1,0:T(8,128)(2,1)}, u32[]{:S(2)}) copy-start(bf16[72,16,128]{2,1,0:T(8,128)(2,1)} %get-tuple-element.213) | copy-start | bytes 884740
  155.1 10.3 %copy-start.47 = (f32[16,256]{1,0:T(8,128)S(1)}, f32[16,256]{1,0:T(8,128)}, u32[]{:S(2)}) copy-start(f32[16,256]{1,0:T(8,128)} %copy-done.46) | copy-start | bytes 49156
  161.8 1.7 collective-permute-start.15
  (1 other events, 0.6 us)
